TPU v7x, 512 devices: a whole 4x8x8 slice. The times are simulated.
512 devices in a mesh: orb: 128 (over z, y, core), grp: 4 (over x).
Axes of the slice: x: 4, y: 8, z: 8, core: 2. Of those that a mesh axis runs over, the one named last changes fastest.
Arguments:
- orbitals: float32 [768, 2, 32, 1024], P('orb', None, 'grp'), may hold values from -6 to 6
- box_offsets: int32 [3, 768], replicated, may hold values from 0 to 191, as said below
- pair_first: int32 [128, 4, 2], P('orb', 'grp'), may hold values from 0 to 767, as said below
- pair_second: int32 [128, 4, 2], P('orb', 'grp'), may hold values from 0 to 767, as said below
- pair_count: int32 [128, 4], P('orb', 'grp'), may hold values from 1 to 2, as said below
Outputs:
- exchange: float32 [768, 2, 32, 1024], P('orb', None, 'grp')
Inputs may be any that keep to these rules, and one draw needn't show every extreme that they name: `box_offsets`: each component of the periodic difference of two orbitals' offsets, taken as in the first step, is under 32 // 2 in magnitude. pair_first[o, g, s] is an orbital of block o, that is of o * 6 to o * 6 + 5. pair_second[o, g, s] is an orbital of block o, not below pair_first, or of block (o + 1) mod 128. Over all live slots every unordered pair stands at most once. `pair_count`: in every block one device has all 2 slots live.
All inputs are finite; a program needn't handle non-finite values.
Results may differ from a plain program's by a relative error of at most 0.0003.
Values sent between devices are 32-bit elements; how exact they have to be, the bound alone decides.
No kernel may reach another device: no remote copies, remote signals or barrier semaphores. Data moves between devices by JAX's collectives and lax.ppermute only.
A program may use at most 64 MiB of HBM per device.

v0:
```python
import jax
import jax.numpy as jnp
from jax import lax
from jax.sharding import PartitionSpec as P

BOX = 32
CELLS = 1024
GRID = 192
ORB_DEV = 6


SCREEN = 0.5
HIGH = lax.Precision.HIGHEST


def from_behind(value, axis, steps):
    count = lax.axis_size(axis)
    pairs = [(source, (source + steps) % count) for source in range(count)]
    return lax.ppermute(value, axis, pairs)


def line_tables():
    index = jnp.arange(BOX, dtype=jnp.int32)
    angle = (index[:, None] * index[None, :] % BOX).astype(jnp.float32) * (2.0 * jnp.pi / BOX)
    return jnp.concatenate([jnp.cos(angle), -jnp.sin(angle)], 0)


def plane_table():
    cell = jnp.arange(CELLS, dtype=jnp.int32)
    ycell = cell // BOX
    zcell = cell % BOX
    phase = (ycell[:, None] * ycell[None, :] + zcell[:, None] * zcell[None, :]) % BOX
    angle = phase.astype(jnp.float32) * (2.0 * jnp.pi / BOX)
    return jnp.concatenate([jnp.cos(angle), -jnp.sin(angle)], 1)


def green_plane():
    modes = jnp.arange(BOX, dtype=jnp.float32)
    lam = (2.0 * jnp.sin(jnp.pi * modes / BOX)) ** 2
    cell = jnp.arange(CELLS, dtype=jnp.int32)
    lam_plane = lam[cell // BOX] + lam[cell % BOX]
    return 1.0 / (SCREEN + lam[:, None] + lam_plane[None, :]) / float(BOX**3)


def combine(product, sign):
    real_part = product[:BOX, :CELLS] - sign * product[BOX:, CELLS:]
    imag_part = product[BOX:, :CELLS] + sign * product[:BOX, CELLS:]
    return (real_part, imag_part)


def along_rows(real_part, imag_part, lines, sign):
    product = jnp.dot(
        lines,
        jnp.concatenate([real_part, imag_part], 1),
        precision=HIGH,
        preferred_element_type=jnp.float32,
    )
    first_re = product[:BOX, :CELLS]
    first_im = product[:BOX, CELLS:]
    second_re = product[BOX:, :CELLS]
    second_im = product[BOX:, CELLS:]
    return (first_re - sign * second_im, first_im + sign * second_re)


def along_plane(real_part, imag_part, plane, sign):
    product = jnp.dot(
        jnp.concatenate([real_part, imag_part], 0),
        plane,
        precision=HIGH,
        preferred_element_type=jnp.float32,
    )
    return combine(product, sign)


def poisson(rho_re, rho_im, lines, plane, green):
    step_re, step_im = along_rows(rho_re, rho_im, lines, 1.0)
    freq_re, freq_im = along_plane(step_re, step_im, plane, 1.0)
    freq_re = green * freq_re
    freq_im = green * freq_im
    back_re, back_im = along_plane(freq_re, freq_im, plane, -1.0)
    return along_rows(back_re, back_im, lines, -1.0)


def carry_box(field, move):
    padded = jnp.pad(field, ((0, 0), (BOX, BOX), (0, 0)))
    rows = lax.dynamic_slice_in_dim(padded, BOX - move[0], BOX, 1)
    wide = jnp.pad(rows, ((0, 0), (0, 0), (CELLS, CELLS)))
    flat = lax.dynamic_slice_in_dim(wide, CELLS - move[1] * BOX - move[2], CELLS, 2)
    cell = jnp.arange(CELLS, dtype=jnp.int32)
    ycell = cell // BOX - move[1]
    zcell = cell % BOX - move[2]
    keep = (ycell >= 0) & (ycell < BOX) & (zcell >= 0) & (zcell < BOX)
    return jnp.where(keep[None, None, :], flat, 0.0)


def local(orbitals, box_offsets, pair_first, pair_second, pair_count):
    own = lax.all_gather(orbitals, "grp", axis=2, tiled=True)
    ahead = from_behind(own, "orb", -1)
    pool = jnp.concatenate([own, ahead], 0)
    lines = line_tables()
    plane = plane_table()
    green = green_plane()
    base = lax.axis_index("orb") * ORB_DEV
    total_orbs = ORB_DEV * lax.axis_size("orb")

    def run_pair(first, second, total):
        local_first = (first - base) % total_orbs
        local_second = (second - base) % total_orbs
        move = (box_offsets[:, second] - box_offsets[:, first] + GRID // 2) % GRID - GRID // 2
        phi_first = pool[local_first]
        moved = carry_box(pool[local_second], move)
        rho_re = moved[0] * phi_first[0] + moved[1] * phi_first[1]
        rho_im = moved[0] * phi_first[1] - moved[1] * phi_first[0]
        pot_re, pot_im = poisson(rho_re, rho_im, lines, plane, green)
        to_first = jnp.stack(
            [moved[0] * pot_re - moved[1] * pot_im, moved[0] * pot_im + moved[1] * pot_re]
        )
        on_first = jnp.stack(
            [
                phi_first[0] * pot_re + phi_first[1] * pot_im,
                phi_first[1] * pot_re - phi_first[0] * pot_im,
            ]
        )
        to_second = carry_box(on_first, -move)
        weight = (first != second).astype(jnp.float32)
        total = total.at[local_first].add(to_first)
        return total.at[local_second].add(weight * to_second)

    start_total = jnp.zeros(pool.shape, jnp.float32)
    firsts = pair_first[0, 0]
    seconds = pair_second[0, 0]

    def own_step(turn, total):
        return run_pair(firsts[turn], seconds[turn], total)

    total = lax.fori_loop(0, pair_count[0, 0], own_step, start_total)
    own_terms = total[:ORB_DEV]
    ahead_terms = total[ORB_DEV:]
    back = from_behind(ahead_terms, "orb", 1)
    summed = lax.psum_scatter(own_terms + back, "grp", scatter_dimension=2, tiled=True)
    return -summed


def solution(mesh):
    placed = (
        P("orb", None, "grp", None),
        P(),
        P("orb", "grp", None),
        P("orb", "grp", None),
        P("orb", "grp"),
    )
    return jax.shard_map(
        local, mesh=mesh, in_specs=placed, out_specs=P("orb", None, "grp", None), check_vma=False
    )
```

profile of v0, /device:TPU:8, one launch (start us, length us, event | category | flops | bytes accessed | tf_op | source)
XLA Modules:
  0.0 246.7 jit_solution(14404542571439244567)
XLA Ops:
  6.5 0.7 all-gather.2.cloned.1.call-update
  7.3 1.6 copy.7
  10.3 0.7 fusion.91
  11.0 4.3 %compare_select_fusion.2 = (f32[1024,1]{0,1:T(1,128)S(1)}, f32[1024,1]{0,1:T(1,128)S(1)}) fusion(f32[]{:T(128)} %bitcast.28, f32[]{:T(128)} %bitcast.29, f32[]{:T(128)} %bitcast.30, f32[]{:T(128)} %bitcast.31, f32[]{:T(128)} %bitcast.32, f32[]{:T(128)} %bitcast.34, f32[]{:T(128)} %bitcast.33), kind=kLoop, calls=%fused_computation.160 | loop fusion | flops 43008 | bytes 8220 | tf_op jit(solution)/shard_map/gather | solution.py:41
  15.4 30.5 %all-gather.2.cloned.1.call-done = f32[6,2,32,1024]{3,2,1,0:T(8,128)} async-done(((f32[6,2,8,1024]{3,2,1,0:T(8,128)}), f32[6,2,32,1024]{3,2,1,0:T(8,128)}) %all-gather.2.cloned.1.call-update) | async-done | bytes 1572880 | tf_op jit(solution)/shard_map/all_gather | solution.py:97
  45.9 1.9 collective-permute-start
  48.9 0.7 fusion.90
  49.6 15.6 %select_add_fusion = f32[1024]{0:T(1024)S(1)} fusion(pred[1024]{0:T(1024)(128)(4,1)S(1)} %compare_reduce_fusion, pred[1024]{0:T(1024)(128)(4,1)S(1)} %compare_reduce_fusion.1, pred[1024]{0:T(1024)(128)(4,1)S(1)} %compare_reduce_fusion.2, pred[1024]{0:T(1024)(128)(4,1)S(1)} %compare_reduce_fusion.3, pred[1024]{0:T(1024)(128)(4,1)S(1)} %compare_reduce_fusion.4, ...), kind=kLoop, calls=%fused_computation.214 | loop fusion | flops 52224 | bytes 63588 | tf_op jit(solution)/shard_map/add | solution.py:41
  65.2 17.1 %fusion.69 = (f32[1024,1024]{1,0:T(8,128)S(1)}, f32[1024,1024]{1,0:T(8,128)S(1)}) fusion(s32[1024]{0:T(1024)S(1)} %get-tuple-element.366, s32[1024]{0:T(1024)S(1)} %get-tuple-element.367), kind=kLoop, calls=%fused_computation.120 | loop fusion | flops 17825792 | bytes 8396800 | tf_op jit(solution)/shard_map/cos | solution.py:34
  82.3 3.8 %pad_maximum_fusion = f32[1024,2048]{1,0:T(8,128)} fusion(f32[1024,1024]{1,0:T(8,128)S(1)} %get-tuple-element.331, f32[1024,1024]{1,0:T(8,128)S(1)} %get-tuple-element.330), kind=kLoop, calls=%fused_computation.111 | loop fusion | flops 2097152 | bytes 16777216 | tf_op jit(solution)/shard_map/concatenate | solution.py:34
  86.1 1.7 pad_maximum_fusion.1
  87.9 2.1 broadcast_in_dim.49
  90.0 90.8 %while.16 = (s32[]{:T(128)}, f32[12,2,32,1024]{3,2,1,0:T(8,128)}, s32[]{:T(128)}, s32[2]{0:T(128)}, s32[]{:T(128)}, /*index=5*/s32[2]{0:T(128)}, s32[3,768]{0,1:...) while((s32[]{:T(128)}, f32[12,2,32,1024]{3,2,1,0:T(8,128)}, ...), condition=%wide.region_3.4_spmd.clone, body=%wide.region_0.3_spmd.clone.sunk | while | flops 3324311552 | bytes 87847112 | solution.py:136
  90.9 1.5 dynamic_slice.135
  94.9 1.3 dynamic_slice.134
  98.3 0.7 fusion.124
  101.8 2.5 %fusion.127 = (pred[1024]{0:T(1024)(128)(4,1)S(1)}, pred[1024]{0:T(1024)(128)(4,1)S(1)}) fusion(s32[]{:T(128)} %bitcast.174, s32[]{:T(128)} %bitcast.175, s32[]{:T(128)} %bitcast.171, s32[]{:T(128)} %bitcast.170), kind=kLoop, calls=%fused_computation.88.clone.1 | loop fusion | flops 30720 | bytes 2064 | tf_op jit(solution)/shard_map/while/body/and | solution.py:92
  106.4 1.0 multiply_add_fusion.2
  107.4 1.3 convolution_bitcast_fusion.4
  108.8 7.7 %fusion.129 = f32[64,2048]{1,0:T(8,128)S(1)} fusion(f32[1024,2048]{1,0:T(8,128)} %get-tuple-element.555, f32[32,1024]{1,0:T(8,128)S(1)} %get-tuple-element.480, f32[32,1024]{1,0:T(8,128)S(1)} %get-tuple-element.481), kind=kOutput, calls=%fused_computation.25.clone.1 | convolution fusion | flops 1610678272 | bytes 9175040 | tf_op jit(solution)/shard_map/while/body/dot_general | solution.py:66
  116.6 5.1 %fusion.131 = f32[64,2048]{1,0:T(8,128)S(1)} fusion(f32[1024,2048]{1,0:T(8,128)S(1)} %copy-done, f32[32,1024]{1,0:T(8,128)S(1)} %get-tuple-element.482, f32[32,1024]{1,0:T(8,128)S(1)} %get-tuple-element.483), kind=kOutput, calls=%fused_computation.29.clone.1 | convolution fusion | flops 1610678272 | bytes 9175040 | tf_op jit(solution)/shard_map/while/body/dot_general | solution.py:66
  121.8 1.3 convolution_bitcast_fusion.5
  123.1 0.7 subtract_bitcast_fusion.4
  123.8 0.8 subtract_bitcast_fusion.5
  126.0 1.0 fusion.134
  127.0 0.8 and_reduce_fusion.3
  127.8 2.3 fusion.133
  132.7 2.5 %fusion.135 = f32[12,2,32,1024]{3,2,1,0:T(8,128)} fusion(f32[12,2,32,1024]{3,2,1,0:T(8,128)} %fusion.133, s32[]{:T(128)} %select_n.608, s32[]{:T(128)S(6)} %select_n.609, f32[2,32,1024]{2,1,0:T(8,128)S(1)} %fusion.134, f32[]{:T(128)S(6)} %convert_element_type.43, pred[1024]{0:T(1024)(128)(4,1)S(1)} %get-tuple-element.494, pred[]{:T(512)} %get-tuple-element.495), kind=kLoop, calls=%fused_computation.11.clone.1 | loop fusion | flops 262144 | bytes 788488 | tf_op jit(solution)/shard_map/while/body/scatter-add | solution.py:127
  135.8 1.5 dynamic_slice.135
  139.9 1.3 dynamic_slice.134
  143.2 0.8 fusion.124
  146.8 2.5 %fusion.127 = (pred[1024]{0:T(1024)(128)(4,1)S(1)}, pred[1024]{0:T(1024)(128)(4,1)S(1)}) fusion(s32[]{:T(128)} %bitcast.174, s32[]{:T(128)} %bitcast.175, s32[]{:T(128)} %bitcast.171, s32[]{:T(128)} %bitcast.170), kind=kLoop, calls=%fused_computation.88.clone.1 | loop fusion | flops 30720 | bytes 2064 | tf_op jit(solution)/shard_map/while/body/and | solution.py:92
  151.4 1.0 multiply_add_fusion.2
  152.4 1.3 convolution_bitcast_fusion.4
  153.8 7.7 %fusion.129 = f32[64,2048]{1,0:T(8,128)S(1)} fusion(f32[1024,2048]{1,0:T(8,128)} %get-tuple-element.555, f32[32,1024]{1,0:T(8,128)S(1)} %get-tuple-element.480, f32[32,1024]{1,0:T(8,128)S(1)} %get-tuple-element.481), kind=kOutput, calls=%fused_computation.25.clone.1 | convolution fusion | flops 1610678272 | bytes 9175040 | tf_op jit(solution)/shard_map/while/body/dot_general | solution.py:66
  161.6 5.1 %fusion.131 = f32[64,2048]{1,0:T(8,128)S(1)} fusion(f32[1024,2048]{1,0:T(8,128)S(1)} %copy-done, f32[32,1024]{1,0:T(8,128)S(1)} %get-tuple-element.482, f32[32,1024]{1,0:T(8,128)S(1)} %get-tuple-element.483), kind=kOutput, calls=%fused_computation.29.clone.1 | convolution fusion | flops 1610678272 | bytes 9175040 | tf_op jit(solution)/shard_map/while/body/dot_general | solution.py:66
  166.8 1.3 convolution_bitcast_fusion.5
  168.8 0.8 subtract_bitcast_fusion.5
  171.0 1.0 fusion.134
  172.0 0.8 and_reduce_fusion.3
  172.8 2.3 fusion.133
  177.7 2.5 %fusion.135 = f32[12,2,32,1024]{3,2,1,0:T(8,128)} fusion(f32[12,2,32,1024]{3,2,1,0:T(8,128)} %fusion.133, s32[]{:T(128)} %select_n.608, s32[]{:T(128)S(6)} %select_n.609, f32[2,32,1024]{2,1,0:T(8,128)S(1)} %fusion.134, f32[]{:T(128)S(6)} %convert_element_type.43, pred[1024]{0:T(1024)(128)(4,1)S(1)} %get-tuple-element.494, pred[]{:T(512)} %get-tuple-element.495), kind=kLoop, calls=%fused_computation.11.clone.1 | loop fusion | flops 262144 | bytes 788488 | tf_op jit(solution)/shard_map/while/body/scatter-add | solution.py:127
  180.8 1.7 slice.255
  182.5 2.4 collective-permute-start.1
  184.9 19.3 %collective-permute-done.1 = f32[6,2,32,1024]{3,2,1,0:T(8,128)S(1)} collective-permute-done((f32[6,2,32,1024]{3,2,1,0:T(8,128)S(1)}, f32[6,2,32,1024]{3,2,1,0:T(8,128)S(1)}, u32[]{:S(2)}, u32[]{:S(2)}) %collective-permute-start.1) | collective-permute-done | bytes 1572896 | tf_op jit(solution)/shard_map/ppermute | solution.py:19
  204.2 1.4 slice_add_fusion.2
  205.6 32.4 %reduce-scatter.2.cloned.1.call-done = f32[6,2,8,1024]{3,2,1,0:T(8,128)} async-done(((f32[6,2,32,1024]{3,2,1,0:T(8,128)}), f32[6,2,8,1024]{3,2,1,0:T(8,128)}) %reduce-scatter.2.cloned.1.call-update) | async-done | bytes 393232 | tf_op jit(solution)/shard_map/reduce_scatter | solution.py:140
  238.1 1.8 neg.18
  (94 shorter events, 6.6 us)
Async XLA Ops:
  6.5 39.4 %all-gather.2.cloned.1.call-start = ((), (), s32[]{:S(2)}) async-start(), calls=%async_computation.1 | async-start | bytes 1966080 | tf_op jit(solution)/shard_map/all_gather | solution.py:97
  7.3 230.8 %reduce-scatter.2.cloned.1.call-start = ((), (), s32[]{:S(2)}) async-start(), calls=%async_computation.2 | async-start | bytes 1966080 | tf_op jit(solution)/shard_map/reduce_scatter | solution.py:140
  45.9 40.2 %collective-permute-start = (f32[6,2,32,1024]{3,2,1,0:T(8,128)}, f32[6,2,32,1024]{3,2,1,0:T(8,128)}, u32[]{:S(2)}, u32[]{:S(2)}) collective-permute-start(f32[6,2,32,1024]{3,2,1,0:T(8,128)} %all-gather.2.cloned.1.call-done), channel_id=1, source_target_pairs={{0,508},{4,0},{8,4},{12,8},{16,12},{20,16},{24,20},{28,24},{32,28}... | collective-permute-start | bytes 4718600 | tf_op jit(solution)/shard_map/ppermute | solution.py:19
  82.3 3.8 %copy-start.4 = (f32[6,2,32,1024]{3,2,1,0:T(8,128)S(1)}, f32[6,2,32,1024]{3,2,1,0:T(8,128)}, u32[]{:S(2)}) copy-start(f32[6,2,32,1024]{3,2,1,0:T(8,128)} %all-gather.2.cloned.1.call-done) | copy-start | bytes 4718596
  86.1 3.9 %copy-start.5 = (s32[4]{0:T(128)S(1)}, s32[4]{0:T(128)}, u32[]{:S(2)}) copy-start(s32[4]{0:T(128)} %constant.269.clone.2) | copy-start | bytes 52
  90.8 10.2 %copy-start.2 = (f32[12,2,32,1024]{3,2,1,0:T(8,128)}, f32[12,2,32,1024]{3,2,1,0:T(8,128)S(1)}, u32[]{:S(2)}) copy-start(f32[12,2,32,1024]{3,2,1,0:T(8,128)S(1)} %get-tuple-element.553) | copy-start | bytes 9437188 | tf_op jit(solution)/shard_map/while
  108.7 7.8 %copy-start = (f32[1024,2048]{1,0:T(8,128)S(1)}, f32[1024,2048]{1,0:T(8,128)}, u32[]{:S(2)}) copy-start(f32[1024,2048]{1,0:T(8,128)} %get-tuple-element.555) | copy-start | bytes 25165828 | tf_op jit(solution)/shard_map/while
  116.6 6.5 %copy-start.3 = (f32[12,2,32,1024]{3,2,1,0:T(8,128)S(1)}, f32[12,2,32,1024]{3,2,1,0:T(8,128)}, u32[]{:S(2)}) copy-start(f32[12,2,32,1024]{3,2,1,0:T(8,128)} %copy-done.2) | copy-start | bytes 9437188 | tf_op jit(solution)/shard_map/while
  135.8 10.3 %copy-start.2 = (f32[12,2,32,1024]{3,2,1,0:T(8,128)}, f32[12,2,32,1024]{3,2,1,0:T(8,128)S(1)}, u32[]{:S(2)}) copy-start(f32[12,2,32,1024]{3,2,1,0:T(8,128)S(1)} %get-tuple-element.553) | copy-start | bytes 9437188 | tf_op jit(solution)/shard_map/while
  153.8 7.8 %copy-start = (f32[1024,2048]{1,0:T(8,128)S(1)}, f32[1024,2048]{1,0:T(8,128)}, u32[]{:S(2)}) copy-start(f32[1024,2048]{1,0:T(8,128)} %get-tuple-element.555) | copy-start | bytes 25165828 | tf_op jit(solution)/shard_map/while
  161.6 6.5 %copy-start.3 = (f32[12,2,32,1024]{3,2,1,0:T(8,128)S(1)}, f32[12,2,32,1024]{3,2,1,0:T(8,128)}, u32[]{:S(2)}) copy-start(f32[12,2,32,1024]{3,2,1,0:T(8,128)} %copy-done.2) | copy-start | bytes 9437188 | tf_op jit(solution)/shard_map/while
  180.8 23.4 %copy-start.1 = (f32[12,2,32,1024]{3,2,1,0:T(8,128)S(1)}, f32[12,2,32,1024]{3,2,1,0:T(8,128)}, u32[]{:S(2)}) copy-start(f32[12,2,32,1024]{3,2,1,0:T(8,128)} %get-tuple-element.226) | copy-start | bytes 9437188
  182.5 21.7 %collective-permute-start.1 = (f32[6,2,32,1024]{3,2,1,0:T(8,128)S(1)}, f32[6,2,32,1024]{3,2,1,0:T(8,128)S(1)}, u32[]{:S(2)}, u32[]{:S(2)}) collective-permute-start(f32[6,2,32,1024]{3,2,1,0:T(8,128)S(1)} %slice.255), channel_id=1, source_target_pairs={{0,4},{4,8},{8,12},{12,16},{16,20},{20,24},{24,28},{28,32},{32,36}... | collective-permute-start | bytes 4718600 | tf_op jit(solution)/shard_map/ppermute | solution.py:19
Sparse Core Ops, SparseCore 0:
  9.5 36.3 all-gather.1
  205.8 32.2 reduce-scatter.1
where the time goes:
time: 248 us; the launch traced here: 247 us
  waiting for transfers between devices  83 us (33%)
  other arithmetic  73.4 us (30%)
  matrix products  30.9 us (12%)
  loops' own time  26.1 us (11%)
  local copies, waits for them, and re-layouts  15.3 us (6%)
  between operations  13.5 us (5%)
  starting transfers between devices  4.34 us (2%)
    reduce_scatter x1, waiting for transfers between devices, local(): lax.psum_scatter(own_terms + back, 'grp', scatter_dimension=2, tiled=True)  32.4 us
    all_gather x1, waiting for transfers between devices, local(): own = lax.all_gather(orbitals, 'grp', axis=2, tiled=True)  30.5 us
    another operation x1, loops' own time, local(): total = lax.fori_loop(0, pair_count[0, 0], own_step, start_total)  26.1 us
    dot_general x4, matrix products, along_plane(): jnp.dot(jnp.concatenate([real_part, imag_part], 0), plane, precision=HIGH...  25.7 us
    ppermute x2, waiting for transfers between devices, from_behind(): return lax.ppermute(value, axis, pairs)  19.3 us
    cos x1, other arithmetic, plane_table(): return jnp.concatenate([jnp.cos(angle), -jnp.sin(angle)], 1)  17.1 us
    add x1, other arithmetic, green_plane(): lam_plane = lam[cell // BOX] + lam[cell % BOX]  15.6 us
    gather x51, other arithmetic, green_plane(): lam_plane = lam[cell // BOX] + lam[cell % BOX]  5.96 us
  transfers between devices with their start and end apart: 4, of which 3 were waited for; matrix products, arithmetic and copies ran while one was open for 19% of the time, Pallas kernels for 0%

commit v1 on v0

v1 whole, which is shorter than its diff:
```python
import jax
import jax.numpy as jnp
import ml_dtypes
import numpy as np
from jax import lax
from jax.experimental import pallas as pl
from jax.experimental.pallas import tpu as pltpu
from jax.sharding import PartitionSpec as P

BOX = 32
CELLS = 1024
GRID = 192
ORB_DEV = 6
PAIRS = 2
SCREEN = 0.5
LANES = 128
SLABS = CELLS // LANES
PARTS = LANES // BOX
ROWS = SLABS * BOX
PAD_SLABS = 4
PAD_ROWS = 16
F32 = jnp.float32
BF16 = jnp.bfloat16


def split_bf16(table):
    high = table.astype(ml_dtypes.bfloat16)
    low = (table - high.astype(np.float64)).astype(ml_dtypes.bfloat16)
    return high, low


def make_tables():
    slab, x = np.divmod(np.arange(ROWS), BOX)
    part, z = np.divmod(np.arange(LANES), BOX)
    left = np.exp(-2j * np.pi * (np.outer(slab, slab) / SLABS + np.outer(x, x) / BOX))
    right = np.exp(-2j * np.pi * (np.outer(part, part) / PARTS + np.outer(z, z) / BOX))
    twiddle = np.exp(-2j * np.pi * np.outer(np.arange(SLABS), part) / BOX)
    left_high, left_low = split_bf16(np.concatenate([left.real, left.imag], 0))
    left3 = np.concatenate([left_high, left_high, left_low], 1)
    forward = np.block([[right.real, right.imag], [-right.imag, right.real]])
    for_high, for_low = split_bf16(forward)
    for3 = np.concatenate([for_high, for_high, for_low], 0)
    back_high, back_low = split_bf16(forward.T)
    back3 = np.concatenate([back_high, back_high, back_low], 0)
    lam = (2.0 * np.sin(np.pi * np.arange(BOX) / BOX)) ** 2
    lam_row = lam[x][:, None]
    lam_y = lam[slab[:, None] + SLABS * part[None, :]]
    green = 1.0 / (SCREEN + lam_row + lam_y + lam[z][None, :]) / float(BOX**3)
    return (
        left3,
        for3,
        back3,
        twiddle.real.astype(np.float32),
        twiddle.imag.astype(np.float32),
        green.astype(np.float32),
    )


TABLES = make_tables()


def from_behind(value, axis, steps):
    count = lax.axis_size(axis)
    pairs = [(source, (source + steps) % count) for source in range(count)]
    return lax.ppermute(value, axis, pairs)


def places(lists, who, turn):
    first = lists[who, turn]
    second = lists[who, PAIRS + turn]
    ahead = (first // ORB_DEV) != (second // ORB_DEV)
    return first % ORB_DEV, second % ORB_DEV, ahead, first != second


def pack_kernel(lists, own, ahead, send, sem):
    members = send.shape[0]
    for who in range(members):
        for turn in range(PAIRS):
            at_first, at_second, is_ahead, _ = places(lists, who, turn)
            pltpu.make_async_copy(own.at[at_first], send.at[who, 2 * turn], sem).start()

            @pl.when(is_ahead)
            def _():
                pltpu.make_async_copy(ahead.at[at_second], send.at[who, 2 * turn + 1], sem).start()

            @pl.when(jnp.logical_not(is_ahead))
            def _():
                pltpu.make_async_copy(own.at[at_second], send.at[who, 2 * turn + 1], sem).start()

    pltpu.make_async_copy(send, send, sem).wait()


def split3(value):
    high = value.astype(BF16)
    low = (value - high.astype(F32)).astype(BF16)
    return high, low


def dot(a, b):
    return jnp.dot(a, b, preferred_element_type=F32)


def left_product(left3, re, im):
    high, low = split3(jnp.concatenate([re, im], 1))
    both = dot(left3[...], jnp.concatenate([high, low, high], 0))
    return both[:ROWS, :LANES], both[:ROWS, LANES:], both[ROWS:, :LANES], both[ROWS:, LANES:]


def right_product(re, im, table):
    high, low = split3(jnp.concatenate([re, im], 1))
    both = dot(jnp.concatenate([high, low, high], 1), table[...])
    return both[:, :LANES], both[:, LANES:]


def by_rows(table):
    return jnp.concatenate(
        [jnp.broadcast_to(table[slab : slab + 1, :], (BOX, LANES)) for slab in range(SLABS)], 0
    )


def poisson(re, im, left3, for3, back3, twid_re, twid_im, green):
    rr, ri, ir, ii = left_product(left3, re, im)
    a_re, a_im = rr - ii, ri + ir
    w_re, w_im = by_rows(twid_re), by_rows(twid_im)
    b_re, b_im = a_re * w_re - a_im * w_im, a_re * w_im + a_im * w_re
    f_re, f_im = right_product(b_re, b_im, for3)
    weight = green[...]
    c_re, c_im = right_product(f_re * weight, f_im * weight, back3)
    d_re, d_im = c_re * w_re + c_im * w_im, c_im * w_re - c_re * w_im
    rr, ri, ir, ii = left_product(left3, d_re, d_im)
    return rr + ii, ri - ir


def shifted(tile_of, buf, move):
    flat = move[1] * BOX + move[2]
    slabs = flat >> 7
    turn = flat & (LANES - 1)
    for comp in range(2):
        for slab in range(SLABS):
            rolled = pltpu.roll(tile_of(comp, slab), turn, 1)
            buf[comp, PAD_SLABS + slab, PAD_ROWS : PAD_ROWS + BOX, :] = rolled
    lane = lax.broadcasted_iota(jnp.int32, (BOX, LANES), 1)
    row = lax.broadcasted_iota(jnp.int32, (BOX, LANES), 0) - move[0]
    zcell = (lane & (BOX - 1)) - move[2]
    part = (lane >> 5) - move[1]
    base = (row >= 0) & (row < BOX) & (zcell >= 0) & (zcell < BOX)
    straight = lane >= turn
    out = []
    for comp in range(2):
        tiles = []
        for slab in range(SLABS + 1):
            tiles.append(buf[comp, PAD_SLABS - 1 + slab - slabs, pl.ds(PAD_ROWS - move[0], BOX), :])
        parts = []
        for slab in range(SLABS):
            ycell = part + slab * PARTS
            keep = base & (ycell >= 0) & (ycell < BOX)
            picked = jnp.where(straight, tiles[slab + 1], tiles[slab])
            parts.append(jnp.where(keep, picked, 0.0))
        out.append(jnp.concatenate(parts, 0))
    return out


def pair_kernel(
    offsets, firsts, seconds, got, left3, for3, back3, twid_re, twid_im, green, send, *bufs
):
    members = got.shape[0]
    height = BOX // members

    def field_tile(slot, comp, slab):
        lanes = slice(slab * LANES, (slab + 1) * LANES)
        return jnp.concatenate([got[who, slot, comp, :, lanes] for who in range(members)], 0)

    def field(slot, comp):
        return jnp.concatenate([field_tile(slot, comp, slab) for slab in range(SLABS)], 0)

    def put(slot, comp, value):
        for slab in range(SLABS):
            for who in range(members):
                at = slab * BOX + who * height
                send[who, slot, comp, :, slab * LANES : (slab + 1) * LANES] = value[at : at + height]

    for turn in range(PAIRS):
        buf = bufs[turn]
        first = firsts[0, 0, turn]
        second = seconds[0, 0, turn]
        move = []
        for axis in range(3):
            gap = offsets[axis, second] - offsets[axis, first] + GRID // 2
            gap = jnp.where(gap < 0, gap + GRID, gap)
            gap = jnp.where(gap >= GRID, gap - GRID, gap)
            move.append(gap - GRID // 2)
        m_re, m_im = shifted(lambda comp, slab: field_tile(2 * turn + 1, comp, slab), buf, move)
        f_re, f_im = field(2 * turn, 0), field(2 * turn, 1)
        rho_re = m_re * f_re + m_im * f_im
        rho_im = m_re * f_im - m_im * f_re
        p_re, p_im = poisson(rho_re, rho_im, left3, for3, back3, twid_re, twid_im, green)
        put(2 * turn, 0, m_re * p_re - m_im * p_im)
        put(2 * turn, 1, m_re * p_im + m_im * p_re)
        back = (f_re * p_re + f_im * p_im, f_im * p_re - f_re * p_im)
        s_re, s_im = shifted(
            lambda comp, slab: back[comp][slab * BOX : (slab + 1) * BOX], buf, [-step for step in move]
        )
        put(2 * turn + 1, 0, s_re)
        put(2 * turn + 1, 1, s_im)


def ahead_kernel(lists, got, out):
    out[...] = jnp.zeros(out.shape, F32)
    for who in range(got.shape[0]):
        for turn in range(PAIRS):
            _, at_second, is_ahead, _ = places(lists, who, turn)

            @pl.when(is_ahead & (turn < lists[who, 2 * PAIRS]))
            def _():
                out[at_second] -= got[who, 2 * turn + 1]


def own_kernel(lists, got, out):
    out[...] = jnp.zeros(out.shape, F32)
    for who in range(got.shape[0]):
        for turn in range(PAIRS):
            at_first, at_second, is_ahead, differs = places(lists, who, turn)
            live = turn < lists[who, 2 * PAIRS]

            @pl.when(live)
            def _():
                out[at_first] -= got[who, 2 * turn]

            @pl.when(live & differs & jnp.logical_not(is_ahead))
            def _():
                out[at_second] -= got[who, 2 * turn + 1]


def local(orbitals, box_offsets, pair_first, pair_second, pair_count):
    members = lax.axis_size("grp")
    rows = orbitals.shape[2]
    smem = pl.BlockSpec(memory_space=pltpu.SMEM)
    vmem = pl.BlockSpec(memory_space=pltpu.VMEM)
    anywhere = pl.BlockSpec(memory_space=pl.ANY)
    limit = pltpu.CompilerParams(vmem_limit_bytes=40 * 1024 * 1024)
    ahead = from_behind(orbitals, "orb", -1)
    mine = jnp.concatenate([pair_first[0, 0], pair_second[0, 0], pair_count[0]])
    lists = lax.all_gather(mine, "grp", axis=0)
    slots = 2 * PAIRS
    fields = jax.ShapeDtypeStruct((members, slots, 2, rows, CELLS), F32)
    packed = pl.pallas_call(
        pack_kernel,
        out_shape=fields,
        in_specs=[smem, anywhere, anywhere],
        out_specs=anywhere,
        scratch_shapes=[pltpu.SemaphoreType.DMA],
        compiler_params=limit,
        name="pack",
    )(lists, orbitals, ahead)
    got = lax.all_to_all(packed, "grp", 0, 0)
    tables = [jnp.asarray(table) for table in TABLES]
    buf = pltpu.VMEM((2, SLABS + 2 * PAD_SLABS, BOX + 2 * PAD_ROWS, LANES), F32)
    terms = pl.pallas_call(
        pair_kernel,
        out_shape=fields,
        in_specs=[smem] * 3 + [vmem] * 7,
        out_specs=vmem,
        scratch_shapes=[buf] * PAIRS,
        compiler_params=limit,
        name="pairs",
    )(box_offsets, pair_first, pair_second, got, *tables)
    returned = lax.all_to_all(terms, "grp", 0, 0)
    shape = jax.ShapeDtypeStruct(orbitals.shape, F32)
    ahead_terms = pl.pallas_call(
        ahead_kernel,
        out_shape=shape,
        in_specs=[smem, vmem],
        out_specs=vmem,
        compiler_params=limit,
        name="ahead_terms",
    )(lists, returned)
    back = from_behind(ahead_terms, "orb", 1)
    own_terms = pl.pallas_call(
        own_kernel,
        out_shape=shape,
        in_specs=[smem, vmem],
        out_specs=vmem,
        compiler_params=limit,
        name="own_terms",
    )(lists, returned)
    return own_terms + back


def solution(mesh):
    placed = (
        P("orb", None, "grp", None),
        P(),
        P("orb", "grp", None),
        P("orb", "grp", None),
        P("orb", "grp"),
    )
    return jax.shard_map(
        local, mesh=mesh, in_specs=placed, out_specs=P("orb", None, "grp", None), check_vma=False
    )
```

time: 248 us -> 72.6 us (0.29)
  the two profiles are of different devices: /device:TPU:8 before, /device:TPU:2 now
where the time goes in v1:
time: 72.6 us; the launch traced here: 72.3 us
  blocking collectives  34.7 us (48%)
  starting transfers between devices  15.2 us (21%)
  waiting for transfers between devices  9.68 us (13%)
  Pallas kernels  7.21 us (10%)
  local copies, waits for them, and re-layouts  3.05 us (4%)
  between operations  1.47 us (2%)
  other arithmetic  0.95 us (1%)
    ppermute x2, starting transfers between devices, from_behind(): return lax.ppermute(value, axis, pairs)  15.2 us
    all_to_all x1, blocking collectives, local(): got = lax.all_to_all(packed, 'grp', 0, 0)  13.4 us
    all_to_all x1, blocking collectives, local(): returned = lax.all_to_all(terms, 'grp', 0, 0)  13.3 us
    ppermute x2, waiting for transfers between devices, from_behind(): return lax.ppermute(value, axis, pairs)  9.68 us
    unnamed x1, blocking collectives  7.98 us
    pallas_call x1, Pallas kernels, local(): pl.pallas_call(pair_kernel, out_shape=fields, in_specs=[smem] * 3 + [vmem...  3.53 us
    unnamed x22, local copies, waits for them, and re-layouts  2.96 us
    pallas_call x1, Pallas kernels, local(): pl.pallas_call(pack_kernel, out_shape=fields, in_specs=[smem, anywhere, a...  2.11 us
  transfers between devices with their start and end apart: 2, of which 1 were waited for; matrix products, arithmetic and copies ran while one was open for 2% of the time, Pallas kernels for 1%

profile of v1, /device:TPU:2, one launch (start us, length us, event | category | flops | bytes accessed | tf_op | source)
XLA Modules:
  0.0 72.3 jit_solution(8018861895063655120)
XLA Ops:
  0.0 13.3 %collective-permute-start = (f32[6,2,8,1024]{3,2,1,0:T(8,128)}, f32[6,2,8,1024]{3,2,1,0:T(8,128)S(1)}, u32[]{:S(2)}, u32[]{:S(2)}) collective-permute-start(f32[6,2,8,1024]{3,2,1,0:T(8,128)} %own.1), channel_id=1, source_target_pairs={{0,508},{4,0},{8,4},{12,8},{16,12},{20,16},{24,20},{28,24},{32,28}... | collective-permute-start | bytes 1179656 | tf_op jit(solution)/shard_map/ppermute | solution.py:65
  13.9 1.3 %dynamic-slice = u32[1]{0:T(128)} dynamic-slice(u32[512]{0:T(512)} %constant.24, u32[]{:T(128)S(6)} %add.4), dynamic_slice_sizes={1} | dynamic-slice | bytes 12
  15.9 0.0 copy-start.8
  15.9 0.0 copy-start.9
  15.9 0.6 copy-done.8
  16.5 0.0 copy-done.9
  16.5 0.2 add_dynamic-update-slice_fusion
  16.7 8.0 %all-reduce = s32[20]{0:T(128)S(1)} all-reduce(s32[20]{0:T(128)S(1)} %add_dynamic-update-slice_fusion), channel_id=2, replica_groups=mesh['orb'=128,'grp'=4] {'grp'}, use_global_device_ids=true, to_apply=%add | all-reduce | flops 20 | bytes 160
  24.7 0.1 reshape.lists
  24.8 0.0 collective-permute-done.ahead
  24.8 0.0 copy-start.3
  24.8 1.0 %copy-done.3 = f32[6,2,8,1024]{3,2,1,0:T(8,128)S(1)} copy-done((f32[6,2,8,1024]{3,2,1,0:T(8,128)S(1)}, f32[6,2,8,1024]{3,2,1,0:T(8,128)}, u32[]{:S(2)}) %copy-start.3) | copy-done | bytes 393240
  25.8 2.1 %pack.1 = f32[4,4,2,8,1024]{4,3,2,1,0:T(8,128)S(1)} custom-call(s32[4,5]{1,0:T(4,128)S(1)} %reshape.lists, f32[6,2,8,1024]{3,2,1,0:T(8,128)S(1)} %copy-done.3, f32[6,2,8,1024]{3,2,1,0:T(8,128)S(1)} %collective-permute-done.ahead), custom_call_target="tpu_custom_call" | custom-call | tf_op jit(solution)/shard_map/pack/pallas_call | solution.py:246
  27.9 0.0 copy-start
  27.9 0.0 copy-start.1
  27.9 0.0 copy-start.2
  27.9 0.0 copy-start.4
  27.9 0.0 copy-start.5
  27.9 0.0 copy-start.6
  28.0 0.0 copy-start.7
  28.0 13.4 %all_to_all.10.got = f32[4,4,2,8,1024]{4,3,2,1,0:T(8,128)S(1)} all-to-all(f32[4,4,2,8,1024]{4,3,2,1,0:T(8,128)S(1)} %pack.1), channel_id=1, replica_groups=mesh['orb'=128,'grp'=4] {'grp'}, dimensions={0} | all-to-all | bytes 2097152 | tf_op jit(solution)/shard_map/all_to_all | solution.py:255
  41.4 0.0 copy-done
  41.4 0.0 copy-done.1
  41.4 0.0 copy-done.2
  41.4 0.0 copy-done.4
  41.4 0.0 copy-done.5
  41.4 0.0 copy-done.6
  41.4 0.0 copy-done.7
  41.4 3.5 %pairs.1 = f32[4,4,2,8,1024]{4,3,2,1,0:T(8,128)S(1)} custom-call(s32[3,768]{1,0:T(4,128)S(1)} %copy-done.5, s32[1,1,2]{2,1,0:T(1,128)S(1)} %copy-done.9, s32[1,1,2]{2,1,0:T(1,128)S(1)} %copy-done.8, f32[4,4,2,8,1024]{4,3,2,1,0:T(8,128)S(1)} %all_to_all.10.got, bf16[512,768]{1,0:T(8,128)(2,1)S(1)} %copy-done, bf16[768,256]{1,0:T(8,128)(2,1)S(1)} %copy-done.2, ...), custom_call_target="tpu_custom_call" | custom-call | tf_op jit(solution)/shard_map/pairs/pallas_call | solution.py:258
  45.0 13.3 %all_to_all.11.got = f32[4,4,2,8,1024]{4,3,2,1,0:T(8,128)S(1)} all-to-all(f32[4,4,2,8,1024]{4,3,2,1,0:T(8,128)S(1)} %pairs.1), channel_id=1, replica_groups=mesh['orb'=128,'grp'=4] {'grp'}, dimensions={0} | all-to-all | bytes 2097152 | tf_op jit(solution)/shard_map/all_to_all | solution.py:267
  58.3 0.8 %ahead_terms.1 = f32[6,2,8,1024]{3,2,1,0:T(8,128)S(1)} custom-call(s32[4,5]{1,0:T(4,128)S(1)} %reshape.lists, f32[4,4,2,8,1024]{4,3,2,1,0:T(8,128)S(1)} %all_to_all.11.got), custom_call_target="tpu_custom_call" | custom-call | tf_op jit(solution)/shard_map/ahead_terms/pallas_call | solution.py:269
  59.1 1.9 %collective-permute-start.1 = (f32[6,2,8,1024]{3,2,1,0:T(8,128)S(1)}, f32[6,2,8,1024]{3,2,1,0:T(8,128)S(1)}, u32[]{:S(2)}, u32[]{:S(2)}) collective-permute-start(f32[6,2,8,1024]{3,2,1,0:T(8,128)S(1)} %ahead_terms.1), channel_id=1, source_target_pairs={{0,4},{4,8},{8,12},{12,16},{16,20},{20,24},{24,28},{28,32},{32,36}... | collective-permute-start | bytes 1179656 | tf_op jit(solution)/shard_map/ppermute | solution.py:65
  61.0 0.8 %own_terms.1 = f32[6,2,8,1024]{3,2,1,0:T(8,128)S(1)} custom-call(s32[4,5]{1,0:T(4,128)S(1)} %reshape.lists, f32[4,4,2,8,1024]{4,3,2,1,0:T(8,128)S(1)} %all_to_all.11.got), custom_call_target="tpu_custom_call" | custom-call | tf_op jit(solution)/shard_map/own_terms/pallas_call | solution.py:278
  61.8 9.7 %collective-permute-done.1 = f32[6,2,8,1024]{3,2,1,0:T(8,128)S(1)} collective-permute-done((f32[6,2,8,1024]{3,2,1,0:T(8,128)S(1)}, f32[6,2,8,1024]{3,2,1,0:T(8,128)S(1)}, u32[]{:S(2)}, u32[]{:S(2)}) %collective-permute-start.1) | collective-permute-done | bytes 393248 | tf_op jit(solution)/shard_map/ppermute | solution.py:65
  71.5 0.8 %add.3 = f32[6,2,8,1024]{3,2,1,0:T(8,128)} add(f32[6,2,8,1024]{3,2,1,0:T(8,128)S(1)} %own_terms.1, f32[6,2,8,1024]{3,2,1,0:T(8,128)S(1)} %collective-permute-done.1) | non-fusion elementwise | flops 98304 | bytes 1179648 | tf_op jit(solution)/shard_map/add | solution.py:286
  (1 shorter events, 0.0 us)
Async XLA Ops:
  0.0 24.8 %collective-permute-start = (f32[6,2,8,1024]{3,2,1,0:T(8,128)}, f32[6,2,8,1024]{3,2,1,0:T(8,128)S(1)}, u32[]{:S(2)}, u32[]{:S(2)}) collective-permute-start(f32[6,2,8,1024]{3,2,1,0:T(8,128)} %own.1), channel_id=1, source_target_pairs={{0,508},{4,0},{8,4},{12,8},{16,12},{20,16},{24,20},{28,24},{32,28}... | collective-permute-start | bytes 1179656 | tf_op jit(solution)/shard_map/ppermute | solution.py:65
  15.9 0.7 copy-start.8
  15.9 0.7 copy-start.9
  24.8 1.0 %copy-start.3 = (f32[6,2,8,1024]{3,2,1,0:T(8,128)S(1)}, f32[6,2,8,1024]{3,2,1,0:T(8,128)}, u32[]{:S(2)}) copy-start(f32[6,2,8,1024]{3,2,1,0:T(8,128)} %own.1) | copy-start | bytes 1179652
  27.9 13.5 %copy-start = (bf16[512,768]{1,0:T(8,128)(2,1)S(1)}, bf16[512,768]{1,0:T(8,128)(2,1)}, u32[]{:S(2)}) copy-start(bf16[512,768]{1,0:T(8,128)(2,1)} %constant.12.clone.left3) | copy-start | bytes 2359300
  27.9 13.5 %copy-start.1 = (bf16[768,256]{1,0:T(8,128)(2,1)S(1)}, bf16[768,256]{1,0:T(8,128)(2,1)}, u32[]{:S(2)}) copy-start(bf16[768,256]{1,0:T(8,128)(2,1)} %constant.14.clone.back3) | copy-start | bytes 1179652
  27.9 13.5 %copy-start.2 = (bf16[768,256]{1,0:T(8,128)(2,1)S(1)}, bf16[768,256]{1,0:T(8,128)(2,1)}, u32[]{:S(2)}) copy-start(bf16[768,256]{1,0:T(8,128)(2,1)} %constant.13.clone.for3) | copy-start | bytes 1179652
  27.9 13.5 %copy-start.4 = (f32[256,128]{1,0:T(8,128)S(1)}, f32[256,128]{1,0:T(8,128)}, u32[]{:S(2)}) copy-start(f32[256,128]{1,0:T(8,128)} %constant.17.clone.green) | copy-start | bytes 393220
  27.9 13.5 %copy-start.5 = (s32[3,768]{1,0:T(4,128)S(1)}, s32[3,768]{1,0:T(4,128)}, u32[]{:S(2)}) copy-start(s32[3,768]{1,0:T(4,128)} %offsets.1) | copy-start | bytes 27652
  27.9 13.5 %copy-start.6 = (f32[8,128]{1,0:T(8,128)S(1)}, f32[8,128]{1,0:T(8,128)}, u32[]{:S(2)}) copy-start(f32[8,128]{1,0:T(8,128)} %constant.16.clone.twid_im) | copy-start | bytes 12292
  28.0 13.5 %copy-start.7 = (f32[8,128]{1,0:T(8,128)S(1)}, f32[8,128]{1,0:T(8,128)}, u32[]{:S(2)}) copy-start(f32[8,128]{1,0:T(8,128)} %constant.15.clone.twid_re) | copy-start | bytes 12292
  59.1 12.4 %collective-permute-start.1 = (f32[6,2,8,1024]{3,2,1,0:T(8,128)S(1)}, f32[6,2,8,1024]{3,2,1,0:T(8,128)S(1)}, u32[]{:S(2)}, u32[]{:S(2)}) collective-permute-start(f32[6,2,8,1024]{3,2,1,0:T(8,128)S(1)} %ahead_terms.1), channel_id=1, source_target_pairs={{0,4},{4,8},{8,12},{12,16},{16,20},{20,24},{24,28},{28,32},{32,36}... | collective-permute-start | bytes 1179656 | tf_op jit(solution)/shard_map/ppermute | solution.py:65

commit v2 on v1

--- a/solution.py
+++ b/solution.py
@@ -65,29 +65,43 @@
     return lax.ppermute(value, axis, pairs)
 
 
+def own_list(pair_first, pair_second, pair_count):
+    spare = LANES - 2 * PAIRS - 1
+    mine = jnp.pad(pair_first, ((0, 0), (0, 0), (0, LANES - PAIRS)))
+    mine += jnp.pad(pair_second, ((0, 0), (0, 0), (PAIRS, LANES - 2 * PAIRS)))
+    mine += jnp.pad(pair_count, ((0, 0), (2 * PAIRS, spare)))[None]
+    return mine
+
+
+def block_lists(mine, members):
+    row = lax.broadcasted_iota(jnp.int32, (members, 1, LANES), 0)
+    return lax.psum(jnp.where(row == lax.axis_index("grp"), mine, 0), "grp")
+
+
 def places(lists, who, turn):
-    first = lists[who, turn]
-    second = lists[who, PAIRS + turn]
+    first = lists[who, 0, turn]
+    second = lists[who, 0, PAIRS + turn]
     ahead = (first // ORB_DEV) != (second // ORB_DEV)
     return first % ORB_DEV, second % ORB_DEV, ahead, first != second
 
 
-def pack_kernel(lists, own, ahead, send, sem):
-    members = send.shape[0]
-    for who in range(members):
+def stage_kernel(source, out):
+    pltpu.sync_copy(source, out)
+
+
+def pack_kernel(lists, behind, here, send):
+    for who in range(send.shape[0]):
         for turn in range(PAIRS):
             at_first, at_second, is_ahead, _ = places(lists, who, turn)
-            pltpu.make_async_copy(own.at[at_first], send.at[who, 2 * turn], sem).start()
+            send[who, 2 * turn] = behind[at_first]
 
             @pl.when(is_ahead)
             def _():
-                pltpu.make_async_copy(ahead.at[at_second], send.at[who, 2 * turn + 1], sem).start()
+                send[who, 2 * turn + 1] = here[at_second]
 
             @pl.when(jnp.logical_not(is_ahead))
             def _():
-                pltpu.make_async_copy(own.at[at_second], send.at[who, 2 * turn + 1], sem).start()
-
-    pltpu.make_async_copy(send, send, sem).wait()
+                send[who, 2 * turn + 1] = behind[at_second]
 
 
 def split3(value):
@@ -161,7 +175,7 @@
 
 
 def pair_kernel(
-    offsets, firsts, seconds, got, left3, for3, back3, twid_re, twid_im, green, send, *bufs
+    offsets, mine, got, left3, for3, back3, twid_re, twid_im, green, send, *bufs
 ):
     members = got.shape[0]
     height = BOX // members
@@ -181,8 +195,8 @@
 
     for turn in range(PAIRS):
         buf = bufs[turn]
-        first = firsts[0, 0, turn]
-        second = seconds[0, 0, turn]
+        first = mine[0, 0, turn]
+        second = mine[0, 0, PAIRS + turn]
         move = []
         for axis in range(3):
             gap = offsets[axis, second] - offsets[axis, first] + GRID // 2
@@ -204,23 +218,23 @@
         put(2 * turn + 1, 1, s_im)
 
 
-def ahead_kernel(lists, got, out):
+def here_kernel(lists, got, out):
     out[...] = jnp.zeros(out.shape, F32)
     for who in range(got.shape[0]):
         for turn in range(PAIRS):
             _, at_second, is_ahead, _ = places(lists, who, turn)
 
-            @pl.when(is_ahead & (turn < lists[who, 2 * PAIRS]))
+            @pl.when(is_ahead & (turn < lists[who, 0, 2 * PAIRS]))
             def _():
                 out[at_second] -= got[who, 2 * turn + 1]
 
 
-def own_kernel(lists, got, out):
+def back_kernel(lists, got, out):
     out[...] = jnp.zeros(out.shape, F32)
     for who in range(got.shape[0]):
         for turn in range(PAIRS):
             at_first, at_second, is_ahead, differs = places(lists, who, turn)
-            live = turn < lists[who, 2 * PAIRS]
+            live = turn < lists[who, 0, 2 * PAIRS]
 
             @pl.when(live)
             def _():
@@ -238,52 +252,59 @@
     vmem = pl.BlockSpec(memory_space=pltpu.VMEM)
     anywhere = pl.BlockSpec(memory_space=pl.ANY)
     limit = pltpu.CompilerParams(vmem_limit_bytes=40 * 1024 * 1024)
-    ahead = from_behind(orbitals, "orb", -1)
-    mine = jnp.concatenate([pair_first[0, 0], pair_second[0, 0], pair_count[0]])
-    lists = lax.all_gather(mine, "grp", axis=0)
+    mine = from_behind(own_list(pair_first, pair_second, pair_count), "orb", 1)
+    here = pl.pallas_call(
+        stage_kernel,
+        out_shape=jax.ShapeDtypeStruct(orbitals.shape, F32),
+        in_specs=[pl.BlockSpec(memory_space=pltpu.HBM)],
+        out_specs=vmem,
+        compiler_params=limit,
+        name="stage",
+    )(pltpu.with_memory_space_constraint(orbitals, pltpu.HBM))
+    behind = from_behind(here, "orb", 1)
+    lists = block_lists(mine, members)
     slots = 2 * PAIRS
     fields = jax.ShapeDtypeStruct((members, slots, 2, rows, CELLS), F32)
     packed = pl.pallas_call(
         pack_kernel,
         out_shape=fields,
-        in_specs=[smem, anywhere, anywhere],
-        out_specs=anywhere,
-        scratch_shapes=[pltpu.SemaphoreType.DMA],
+        in_specs=[smem, vmem, vmem],
+        out_specs=vmem,
         compiler_params=limit,
         name="pack",
-    )(lists, orbitals, ahead)
+    )(lists, behind, here)
     got = lax.all_to_all(packed, "grp", 0, 0)
     tables = [jnp.asarray(table) for table in TABLES]
     buf = pltpu.VMEM((2, SLABS + 2 * PAD_SLABS, BOX + 2 * PAD_ROWS, LANES), F32)
     terms = pl.pallas_call(
         pair_kernel,
         out_shape=fields,
-        in_specs=[smem] * 3 + [vmem] * 7,
+        in_specs=[smem] * 2 + [vmem] * 7,
         out_specs=vmem,
         scratch_shapes=[buf] * PAIRS,
         compiler_params=limit,
         name="pairs",
-    )(box_offsets, pair_first, pair_second, got, *tables)
+    )(box_offsets, mine, got, *tables)
     returned = lax.all_to_all(terms, "grp", 0, 0)
     shape = jax.ShapeDtypeStruct(orbitals.shape, F32)
-    ahead_terms = pl.pallas_call(
-        ahead_kernel,
+    back_terms = pl.pallas_call(
+        back_kernel,
         out_shape=shape,
         in_specs=[smem, vmem],
         out_specs=vmem,
         compiler_params=limit,
-        name="ahead_terms",
+        name="back_terms",
     )(lists, returned)
-    back = from_behind(ahead_terms, "orb", 1)
-    own_terms = pl.pallas_call(
-        own_kernel,
+    back = from_behind(back_terms, "orb", -1)
+    here_terms = pl.pallas_call(
+        here_kernel,
         out_shape=shape,
         in_specs=[smem, vmem],
         out_specs=vmem,
         compiler_params=limit,
-        name="own_terms",
+        name="here_terms",
     )(lists, returned)
-    return own_terms + back
+    return here_terms + back
 
 
 def solution(mesh):

time: 72.6 us -> 69.9 us (0.963)
  starting transfers between devices: 15.2 us -> 7.54 us
  waiting for transfers between devices: 9.68 us -> 17 us
  local copies, waits for them, and re-layouts: 3.05 us -> 0.05 us
  blocking collectives: 34.7 us -> 36.3 us
    psum x0 -> x1, blocking collectives: none -> 8.1 us  [block_lists(): return lax.psum(jnp.where(row == lax.axis_index('grp'), mine, 0), 'grp')]
    unnamed x1 -> x0, blocking collectives: 7.98 us -> none
    ppermute x2 -> x3, starting transfers between devices: 15.2 us -> 7.54 us  [from_behind(): return lax.ppermute(value, axis, pairs)]
    ppermute x2 -> x3, waiting for transfers between devices: 9.68 us -> 17 us  [from_behind(): return lax.ppermute(value, axis, pairs)]
    unnamed x22 -> x18, local copies, waits for them, and re-layouts: 2.96 us -> 0.05 us
    all_to_all x1, blocking collectives: 13.4 us -> 15 us  [local(): got = lax.all_to_all(packed, 'grp', 0, 0)]
    pallas_call x4 -> x5, Pallas kernels: 7.21 us -> 6.84 us  [the longest x1 3.5 us: local(): pl.pallas_call(pair_kernel, out_shape=fields, in_specs=[smem] * 2 + [vmem...]
  transfers between devices with their start and end apart: 2 -> 3, of which waited for: 1 -> 2; matrix products, arithmetic and copies ran while one was open for 2% -> 0% of each run, Pallas kernels for 1% -> 1%
where the time goes in v2:
time: 69.9 us; the launch traced here: 69.6 us
  blocking collectives  36.3 us (52%)
  waiting for transfers between devices  17 us (24%)
  starting transfers between devices  7.54 us (11%)
  Pallas kernels  6.84 us (10%)
  other arithmetic  0.94 us (1%)
  between operations  0.83 us (1%)
    ppermute x3, waiting for transfers between devices, from_behind(): return lax.ppermute(value, axis, pairs)  17 us
    all_to_all x1, blocking collectives, local(): got = lax.all_to_all(packed, 'grp', 0, 0)  15 us
    all_to_all x1, blocking collectives, local(): returned = lax.all_to_all(terms, 'grp', 0, 0)  13.3 us
    psum x1, blocking collectives, block_lists(): return lax.psum(jnp.where(row == lax.axis_index('grp'), mine, 0), 'grp')  8.1 us
    ppermute x3, starting transfers between devices, from_behind(): return lax.ppermute(value, axis, pairs)  7.54 us
    pallas_call x1, Pallas kernels, local(): pl.pallas_call(pair_kernel, out_shape=fields, in_specs=[smem] * 2 + [vmem...  3.5 us
  transfers between devices with their start and end apart: 3, of which 2 were waited for; matrix products, arithmetic and copies ran while one was open for 0% of the time, Pallas kernels for 1%

profile of v2, /device:TPU:2, one launch (start us, length us, event | category | flops | bytes accessed | tf_op | source)
XLA Modules:
  0.0 69.6 jit_solution(9214577622491786275)
XLA Ops:
  0.0 1.0 %stage.1.here = f32[6,2,8,1024]{3,2,1,0:T(8,128)S(1)} custom-call(f32[6,2,8,1024]{3,2,1,0:T(8,128)} %source.1), custom_call_target="tpu_custom_call" | custom-call | tf_op jit(solution)/shard_map/stage/pallas_call | solution.py:256
  1.0 0.0 copy-start.7
  1.0 0.0 copy-start.8
  1.0 2.0 %collective-permute-start.1 = (f32[6,2,8,1024]{3,2,1,0:T(8,128)S(1)}, f32[6,2,8,1024]{3,2,1,0:T(8,128)S(1)}, u32[]{:S(2)}, u32[]{:S(2)}) collective-permute-start(f32[6,2,8,1024]{3,2,1,0:T(8,128)S(1)} %stage.1.here), channel_id=1, source_target_pairs={{0,4},{4,8},{8,12},{12,16},{16,20},{20,24},{24,28},{28,32},{32,36}... | collective-permute-start | bytes 1179656 | tf_op jit(solution)/shard_map/ppermute | solution.py:65
  3.7 0.0 copy-done.7
  3.7 0.0 copy-done.8
  3.7 0.1 bitcast_add_fusion
  3.8 3.6 %collective-permute-start = (s32[1,1,128]{2,1,0:T(1,128)S(1)}, s32[1,1,128]{2,1,0:T(1,128)S(1)}, u32[]{:S(2)}, u32[]{:S(2)}) collective-permute-start(s32[1,1,128]{2,1,0:T(1,128)S(1)} %bitcast_add_fusion), channel_id=1, source_target_pairs={{0,4},{4,8},{8,12},{12,16},{16,20},{20,24},{24,28},{28,32},{32,36}... | collective-permute-start | bytes 1544 | tf_op jit(solution)/shard_map/ppermute | solution.py:65
  7.4 12.5 %collective-permute-done.mine = s32[1,1,128]{2,1,0:T(1,128)S(1)} collective-permute-done((s32[1,1,128]{2,1,0:T(1,128)S(1)}, s32[1,1,128]{2,1,0:T(1,128)S(1)}, u32[]{:S(2)}, u32[]{:S(2)}) %collective-permute-start) | collective-permute-done | bytes 544 | tf_op jit(solution)/shard_map/ppermute | solution.py:65
  19.9 0.1 broadcast_select_fusion
  20.0 8.1 %psum.7.lists = s32[4,1,128]{2,1,0:T(1,128)S(1)} all-reduce(s32[4,1,128]{2,1,0:T(1,128)S(1)} %broadcast_select_fusion), channel_id=1, replica_groups=mesh['orb'=128,'grp'=4] {'grp'}, use_global_device_ids=true, to_apply=%region_0.1 | all-reduce | flops 512 | bytes 4096 | tf_op jit(solution)/shard_map/psum | solution.py:78
  28.1 0.0 collective-permute-done.1.behind
  28.1 0.8 %pack.1 = f32[4,4,2,8,1024]{4,3,2,1,0:T(8,128)S(1)} custom-call(s32[4,1,128]{2,1,0:T(1,128)S(1)} %psum.7.lists, f32[6,2,8,1024]{3,2,1,0:T(8,128)S(1)} %collective-permute-done.1.behind, f32[6,2,8,1024]{3,2,1,0:T(8,128)S(1)} %stage.1.here), custom_call_target="tpu_custom_call" | custom-call | tf_op jit(solution)/shard_map/pack/pallas_call | solution.py:268
  28.9 0.0 copy-start
  28.9 0.0 copy-start.1
  28.9 0.0 copy-start.2
  28.9 0.0 copy-start.3
  29.0 0.0 copy-start.4
  29.0 0.0 copy-start.5
  29.0 0.0 copy-start.6
  29.0 15.0 %all_to_all.10.got = f32[4,4,2,8,1024]{4,3,2,1,0:T(8,128)S(1)} all-to-all(f32[4,4,2,8,1024]{4,3,2,1,0:T(8,128)S(1)} %pack.1), channel_id=1, replica_groups=mesh['orb'=128,'grp'=4] {'grp'}, dimensions={0} | all-to-all | bytes 2097152 | tf_op jit(solution)/shard_map/all_to_all | solution.py:276
  44.0 0.0 copy-done
  44.0 0.0 copy-done.1
  44.0 0.0 copy-done.2
  44.0 0.0 copy-done.3
  44.0 0.0 copy-done.4
  44.0 0.0 copy-done.5
  44.0 0.0 copy-done.6
  44.0 3.5 %pairs.1 = f32[4,4,2,8,1024]{4,3,2,1,0:T(8,128)S(1)} custom-call(s32[3,768]{1,0:T(4,128)S(1)} %copy-done.4, s32[1,1,128]{2,1,0:T(1,128)S(1)} %collective-permute-done.mine, f32[4,4,2,8,1024]{4,3,2,1,0:T(8,128)S(1)} %all_to_all.10.got, bf16[512,768]{1,0:T(8,128)(2,1)S(1)} %copy-done, bf16[768,256]{1,0:T(8,128)(2,1)S(1)} %copy-done.2, ...), custom_call_target="tpu_custom_call" | custom-call | tf_op jit(solution)/shard_map/pairs/pallas_call | solution.py:279
  47.5 13.3 %all_to_all.11.got = f32[4,4,2,8,1024]{4,3,2,1,0:T(8,128)S(1)} all-to-all(f32[4,4,2,8,1024]{4,3,2,1,0:T(8,128)S(1)} %pairs.1), channel_id=1, replica_groups=mesh['orb'=128,'grp'=4] {'grp'}, dimensions={0} | all-to-all | bytes 2097152 | tf_op jit(solution)/shard_map/all_to_all | solution.py:288
  60.8 0.8 %back_terms.1 = f32[6,2,8,1024]{3,2,1,0:T(8,128)S(1)} custom-call(s32[4,1,128]{2,1,0:T(1,128)S(1)} %psum.7.lists, f32[4,4,2,8,1024]{4,3,2,1,0:T(8,128)S(1)} %all_to_all.11.got), custom_call_target="tpu_custom_call" | custom-call | tf_op jit(solution)/shard_map/back_terms/pallas_call | solution.py:290
  61.6 1.9 %collective-permute-start.2 = (f32[6,2,8,1024]{3,2,1,0:T(8,128)S(1)}, f32[6,2,8,1024]{3,2,1,0:T(8,128)S(1)}, u32[]{:S(2)}, u32[]{:S(2)}) collective-permute-start(f32[6,2,8,1024]{3,2,1,0:T(8,128)S(1)} %back_terms.1), channel_id=1, source_target_pairs={{0,508},{4,0},{8,4},{12,8},{16,12},{20,16},{24,20},{28,24},{32,28}... | collective-permute-start | bytes 1179656 | tf_op jit(solution)/shard_map/ppermute | solution.py:65
  63.5 0.8 %here_terms.1 = f32[6,2,8,1024]{3,2,1,0:T(8,128)S(1)} custom-call(s32[4,1,128]{2,1,0:T(1,128)S(1)} %psum.7.lists, f32[4,4,2,8,1024]{4,3,2,1,0:T(8,128)S(1)} %all_to_all.11.got), custom_call_target="tpu_custom_call" | custom-call | tf_op jit(solution)/shard_map/here_terms/pallas_call | solution.py:299
  64.3 4.5 %collective-permute-done.2 = f32[6,2,8,1024]{3,2,1,0:T(8,128)S(1)} collective-permute-done((f32[6,2,8,1024]{3,2,1,0:T(8,128)S(1)}, f32[6,2,8,1024]{3,2,1,0:T(8,128)S(1)}, u32[]{:S(2)}, u32[]{:S(2)}) %collective-permute-start.2) | collective-permute-done | bytes 393248 | tf_op jit(solution)/shard_map/ppermute | solution.py:65
  68.8 0.8 %add.19 = f32[6,2,8,1024]{3,2,1,0:T(8,128)} add(f32[6,2,8,1024]{3,2,1,0:T(8,128)S(1)} %here_terms.1, f32[6,2,8,1024]{3,2,1,0:T(8,128)S(1)} %collective-permute-done.2) | non-fusion elementwise | flops 98304 | bytes 1179648 | tf_op jit(solution)/shard_map/add | solution.py:307
  (1 shorter events, 0.0 us)
Async XLA Ops:
  1.0 2.7 %copy-start.7 = (s32[1,1,2]{2,1,0:T(1,128)S(1)}, s32[1,1,2]{2,1,0:T(1,128)}, u32[]{:S(2)}) copy-start(s32[1,1,2]{2,1,0:T(1,128)} %param.14) | copy-start | bytes 28
  1.0 2.7 %copy-start.8 = (s32[1,1,2]{2,1,0:T(1,128)S(1)}, s32[1,1,2]{2,1,0:T(1,128)}, u32[]{:S(2)}) copy-start(s32[1,1,2]{2,1,0:T(1,128)} %param.13) | copy-start | bytes 28
  1.0 27.1 %collective-permute-start.1 = (f32[6,2,8,1024]{3,2,1,0:T(8,128)S(1)}, f32[6,2,8,1024]{3,2,1,0:T(8,128)S(1)}, u32[]{:S(2)}, u32[]{:S(2)}) collective-permute-start(f32[6,2,8,1024]{3,2,1,0:T(8,128)S(1)} %stage.1.here), channel_id=1, source_target_pairs={{0,4},{4,8},{8,12},{12,16},{16,20},{20,24},{24,28},{28,32},{32,36}... | collective-permute-start | bytes 1179656 | tf_op jit(solution)/shard_map/ppermute | solution.py:65
  3.8 16.1 %collective-permute-start = (s32[1,1,128]{2,1,0:T(1,128)S(1)}, s32[1,1,128]{2,1,0:T(1,128)S(1)}, u32[]{:S(2)}, u32[]{:S(2)}) collective-permute-start(s32[1,1,128]{2,1,0:T(1,128)S(1)} %bitcast_add_fusion), channel_id=1, source_target_pairs={{0,4},{4,8},{8,12},{12,16},{16,20},{20,24},{24,28},{28,32},{32,36}... | collective-permute-start | bytes 1544 | tf_op jit(solution)/shard_map/ppermute | solution.py:65
  28.9 15.1 %copy-start = (bf16[512,768]{1,0:T(8,128)(2,1)S(1)}, bf16[512,768]{1,0:T(8,128)(2,1)}, u32[]{:S(2)}) copy-start(bf16[512,768]{1,0:T(8,128)(2,1)} %constant.18.clone.left3) | copy-start | bytes 2359300
  28.9 15.0 %copy-start.1 = (bf16[768,256]{1,0:T(8,128)(2,1)S(1)}, bf16[768,256]{1,0:T(8,128)(2,1)}, u32[]{:S(2)}) copy-start(bf16[768,256]{1,0:T(8,128)(2,1)} %constant.20.clone.back3) | copy-start | bytes 1179652
  28.9 15.0 %copy-start.2 = (bf16[768,256]{1,0:T(8,128)(2,1)S(1)}, bf16[768,256]{1,0:T(8,128)(2,1)}, u32[]{:S(2)}) copy-start(bf16[768,256]{1,0:T(8,128)(2,1)} %constant.19.clone.for3) | copy-start | bytes 1179652
  28.9 15.0 %copy-start.3 = (f32[256,128]{1,0:T(8,128)S(1)}, f32[256,128]{1,0:T(8,128)}, u32[]{:S(2)}) copy-start(f32[256,128]{1,0:T(8,128)} %constant.23.clone.green) | copy-start | bytes 393220
  29.0 15.0 %copy-start.4 = (s32[3,768]{1,0:T(4,128)S(1)}, s32[3,768]{1,0:T(4,128)}, u32[]{:S(2)}) copy-start(s32[3,768]{1,0:T(4,128)} %offsets.1) | copy-start | bytes 27652
  29.0 15.0 %copy-start.5 = (f32[8,128]{1,0:T(8,128)S(1)}, f32[8,128]{1,0:T(8,128)}, u32[]{:S(2)}) copy-start(f32[8,128]{1,0:T(8,128)} %constant.22.clone.twid_im) | copy-start | bytes 12292
  29.0 15.0 %copy-start.6 = (f32[8,128]{1,0:T(8,128)S(1)}, f32[8,128]{1,0:T(8,128)}, u32[]{:S(2)}) copy-start(f32[8,128]{1,0:T(8,128)} %constant.21.clone.twid_re) | copy-start | bytes 12292
  61.6 7.2 %collective-permute-start.2 = (f32[6,2,8,1024]{3,2,1,0:T(8,128)S(1)}, f32[6,2,8,1024]{3,2,1,0:T(8,128)S(1)}, u32[]{:S(2)}, u32[]{:S(2)}) collective-permute-start(f32[6,2,8,1024]{3,2,1,0:T(8,128)S(1)} %back_terms.1), channel_id=1, source_target_pairs={{0,508},{4,0},{8,4},{12,8},{16,12},{20,16},{24,20},{28,24},{32,28}... | collective-permute-start | bytes 1179656 | tf_op jit(solution)/shard_map/ppermute | solution.py:65

commit v3 on v2

--- a/solution.py
+++ b/solution.py
@@ -32,7 +32,7 @@
 def make_tables():
     slab, x = np.divmod(np.arange(ROWS), BOX)
     part, z = np.divmod(np.arange(LANES), BOX)
-    left = np.exp(-2j * np.pi * (np.outer(slab, slab) / SLABS + np.outer(x, x) / BOX))
+    left = np.exp(-2j * np.pi * np.outer(np.arange(BOX), np.arange(BOX)) / BOX)
     right = np.exp(-2j * np.pi * (np.outer(part, part) / PARTS + np.outer(z, z) / BOX))
     twiddle = np.exp(-2j * np.pi * np.outer(np.arange(SLABS), part) / BOX)
     left_high, left_low = split_bf16(np.concatenate([left.real, left.imag], 0))
@@ -65,19 +65,6 @@
     return lax.ppermute(value, axis, pairs)
 
 
-def own_list(pair_first, pair_second, pair_count):
-    spare = LANES - 2 * PAIRS - 1
-    mine = jnp.pad(pair_first, ((0, 0), (0, 0), (0, LANES - PAIRS)))
-    mine += jnp.pad(pair_second, ((0, 0), (0, 0), (PAIRS, LANES - 2 * PAIRS)))
-    mine += jnp.pad(pair_count, ((0, 0), (2 * PAIRS, spare)))[None]
-    return mine
-
-
-def block_lists(mine, members):
-    row = lax.broadcasted_iota(jnp.int32, (members, 1, LANES), 0)
-    return lax.psum(jnp.where(row == lax.axis_index("grp"), mine, 0), "grp")
-
-
 def places(lists, who, turn):
     first = lists[who, 0, turn]
     second = lists[who, 0, PAIRS + turn]
@@ -85,20 +72,36 @@
     return first % ORB_DEV, second % ORB_DEV, ahead, first != second
 
 
-def stage_kernel(source, out):
-    pltpu.sync_copy(source, out)
-
-
-def pack_kernel(lists, behind, here, send):
+def entry_kernel(firsts, seconds, count, rows, table, here, sem):
+    copy = pltpu.make_async_copy(rows, here, sem)
+    copy.start()
+    who = lax.broadcasted_iota(jnp.int32, table.shape, 0)
+    lane = lax.broadcasted_iota(jnp.int32, table.shape, 2)
+    value = jnp.where(lane == 2 * PAIRS, count[0, 0], 0)
+    for turn in range(PAIRS):
+        value = jnp.where(lane == turn, firsts[0, 0, turn], value)
+        value = jnp.where(lane == PAIRS + turn, seconds[0, 0, turn], value)
+    table[...] = jnp.where(who == lax.axis_index("grp"), value, 0)
+    copy.wait()
+
+
+def pack_here_kernel(lists, here, send):
+    for who in range(send.shape[0]):
+        for turn in range(PAIRS):
+            _, at_second, is_ahead, _ = places(lists, who, turn)
+
+            @pl.when(is_ahead)
+            def _():
+                send[who, 2 * turn + 1] = here[at_second]
+
+
+def pack_behind_kernel(lists, behind, packed, send):
+    del packed
     for who in range(send.shape[0]):
         for turn in range(PAIRS):
             at_first, at_second, is_ahead, _ = places(lists, who, turn)
             send[who, 2 * turn] = behind[at_first]
 
-            @pl.when(is_ahead)
-            def _():
-                send[who, 2 * turn + 1] = here[at_second]
-
             @pl.when(jnp.logical_not(is_ahead))
             def _():
                 send[who, 2 * turn + 1] = behind[at_second]
@@ -114,10 +117,48 @@
     return jnp.dot(a, b, preferred_element_type=F32)
 
 
-def left_product(left3, re, im):
-    high, low = split3(jnp.concatenate([re, im], 1))
+def fourth(a, b, c, d, sign):
+    s_re, s_im, t_re, t_im = a[0] + c[0], a[1] + c[1], a[0] - c[0], a[1] - c[1]
+    u_re, u_im, v_re, v_im = b[0] + d[0], b[1] + d[1], b[0] - d[0], b[1] - d[1]
+    w_re, w_im = -sign * v_im, sign * v_re
+    return (
+        (s_re + u_re, s_im + u_im),
+        (t_re + w_re, t_im + w_im),
+        (s_re - u_re, s_im - u_im),
+        (t_re - w_re, t_im - w_im),
+    )
+
+
+def eighth(x, sign):
+    low = [(x[k][0] + x[k + 4][0], x[k][1] + x[k + 4][1]) for k in range(4)]
+    high = [(x[k][0] - x[k + 4][0], x[k][1] - x[k + 4][1]) for k in range(4)]
+    half = np.float32(np.sqrt(0.5))
+    turned = [
+        high[0],
+        (half * (high[1][0] - sign * high[1][1]), half * (high[1][1] + sign * high[1][0])),
+        (-sign * high[2][1], sign * high[2][0]),
+        (-half * (high[3][0] + sign * high[3][1]), half * (sign * high[3][0] - high[3][1])),
+    ]
+    even = fourth(*low, sign)
+    odd = fourth(*turned, sign)
+    return [even[k // 2] if k % 2 == 0 else odd[k // 2] for k in range(SLABS)]
+
+
+def slab_tiles(re, im):
+    count = re.shape[0] // BOX
+    return [(re[s * BOX : (s + 1) * BOX], im[s * BOX : (s + 1) * BOX]) for s in range(count)]
+
+
+def along_x(left3, tiles, sign):
+    wide = jnp.concatenate([part for tile in tiles for part in tile], 1)
+    high, low = split3(wide)
     both = dot(left3[...], jnp.concatenate([high, low, high], 0))
-    return both[:ROWS, :LANES], both[:ROWS, LANES:], both[ROWS:, :LANES], both[ROWS:, LANES:]
+    re, im = [], []
+    for s in range(len(tiles)):
+        a, b = slice(2 * s * LANES, (2 * s + 1) * LANES), slice((2 * s + 1) * LANES, (2 * s + 2) * LANES)
+        re.append(both[:BOX, a] + sign * both[BOX:, b])
+        im.append(both[:BOX, b] - sign * both[BOX:, a])
+    return re, im
 
 
 def right_product(re, im, table):
@@ -132,17 +173,25 @@
     )
 
 
-def poisson(re, im, left3, for3, back3, twid_re, twid_im, green):
-    rr, ri, ir, ii = left_product(left3, re, im)
-    a_re, a_im = rr - ii, ri + ir
-    w_re, w_im = by_rows(twid_re), by_rows(twid_im)
+def poisson(rhos, left3, for3, back3, twid_re, twid_im, green):
+    count = len(rhos)
+    tiles = [tile for re, im in rhos for tile in eighth(slab_tiles(re, im), -1.0)]
+    a_re, a_im = along_x(left3, tiles, -1.0)
+    a_re, a_im = jnp.concatenate(a_re, 0), jnp.concatenate(a_im, 0)
+    w_re = jnp.concatenate([by_rows(twid_re)] * count, 0)
+    w_im = jnp.concatenate([by_rows(twid_im)] * count, 0)
     b_re, b_im = a_re * w_re - a_im * w_im, a_re * w_im + a_im * w_re
     f_re, f_im = right_product(b_re, b_im, for3)
-    weight = green[...]
+    weight = jnp.concatenate([green[...]] * count, 0)
     c_re, c_im = right_product(f_re * weight, f_im * weight, back3)
     d_re, d_im = c_re * w_re + c_im * w_im, c_im * w_re - c_re * w_im
-    rr, ri, ir, ii = left_product(left3, d_re, d_im)
-    return rr + ii, ri - ir
+    e_re, e_im = along_x(left3, slab_tiles(d_re, d_im), 1.0)
+    out = []
+    for at in range(count):
+        picked = slice(at * SLABS, (at + 1) * SLABS)
+        tiles = eighth(list(zip(e_re[picked], e_im[picked])), 1.0)
+        out.append(tuple(jnp.concatenate([tile[k] for tile in tiles], 0) for k in range(2)))
+    return out
 
 
 def shifted(tile_of, buf, move):
@@ -175,10 +224,11 @@
 
 
 def pair_kernel(
-    offsets, mine, got, left3, for3, back3, twid_re, twid_im, green, send, *bufs
+    offsets, lists, got, left3, for3, back3, twid_re, twid_im, green, send, *bufs
 ):
     members = got.shape[0]
     height = BOX // members
+    me = lax.axis_index("grp")
 
     def field_tile(slot, comp, slab):
         lanes = slice(slab * LANES, (slab + 1) * LANES)
@@ -193,26 +243,34 @@
                 at = slab * BOX + who * height
                 send[who, slot, comp, :, slab * LANES : (slab + 1) * LANES] = value[at : at + height]
 
+    moves, moved, firsts, rhos = [], [], [], []
     for turn in range(PAIRS):
-        buf = bufs[turn]
-        first = mine[0, 0, turn]
-        second = mine[0, 0, PAIRS + turn]
+        first = lists[me, 0, turn]
+        second = lists[me, 0, PAIRS + turn]
         move = []
         for axis in range(3):
             gap = offsets[axis, second] - offsets[axis, first] + GRID // 2
             gap = jnp.where(gap < 0, gap + GRID, gap)
             gap = jnp.where(gap >= GRID, gap - GRID, gap)
             move.append(gap - GRID // 2)
-        m_re, m_im = shifted(lambda comp, slab: field_tile(2 * turn + 1, comp, slab), buf, move)
+        moves.append(move)
+        m_re, m_im = shifted(
+            lambda comp, slab: field_tile(2 * turn + 1, comp, slab), bufs[turn], move
+        )
         f_re, f_im = field(2 * turn, 0), field(2 * turn, 1)
-        rho_re = m_re * f_re + m_im * f_im
-        rho_im = m_re * f_im - m_im * f_re
-        p_re, p_im = poisson(rho_re, rho_im, left3, for3, back3, twid_re, twid_im, green)
+        moved.append((m_re, m_im))
+        firsts.append((f_re, f_im))
+        rhos.append((m_re * f_re + m_im * f_im, m_re * f_im - m_im * f_re))
+    pots = poisson(rhos, left3, for3, back3, twid_re, twid_im, green)
+    for turn in range(PAIRS):
+        (m_re, m_im), (f_re, f_im), (p_re, p_im) = moved[turn], firsts[turn], pots[turn]
         put(2 * turn, 0, m_re * p_re - m_im * p_im)
         put(2 * turn, 1, m_re * p_im + m_im * p_re)
         back = (f_re * p_re + f_im * p_im, f_im * p_re - f_re * p_im)
         s_re, s_im = shifted(
-            lambda comp, slab: back[comp][slab * BOX : (slab + 1) * BOX], buf, [-step for step in move]
+            lambda comp, slab: back[comp][slab * BOX : (slab + 1) * BOX],
+            bufs[turn],
+            [-step for step in moves[turn]],
         )
         put(2 * turn + 1, 0, s_re)
         put(2 * turn + 1, 1, s_im)
@@ -252,27 +310,46 @@
     vmem = pl.BlockSpec(memory_space=pltpu.VMEM)
     anywhere = pl.BlockSpec(memory_space=pl.ANY)
     limit = pltpu.CompilerParams(vmem_limit_bytes=40 * 1024 * 1024)
-    mine = from_behind(own_list(pair_first, pair_second, pair_count), "orb", 1)
-    here = pl.pallas_call(
-        stage_kernel,
-        out_shape=jax.ShapeDtypeStruct(orbitals.shape, F32),
-        in_specs=[pl.BlockSpec(memory_space=pltpu.HBM)],
-        out_specs=vmem,
-        compiler_params=limit,
-        name="stage",
-    )(pltpu.with_memory_space_constraint(orbitals, pltpu.HBM))
+    mine, here = pl.pallas_call(
+        entry_kernel,
+        out_shape=(
+            jax.ShapeDtypeStruct((members, 1, LANES), jnp.int32),
+            jax.ShapeDtypeStruct(orbitals.shape, F32),
+        ),
+        in_specs=[smem] * 3 + [pl.BlockSpec(memory_space=pltpu.HBM)],
+        out_specs=(vmem, vmem),
+        scratch_shapes=[pltpu.SemaphoreType.DMA],
+        compiler_params=limit,
+        name="entry",
+    )(
+        pair_first,
+        pair_second,
+        pair_count,
+        pltpu.with_memory_space_constraint(orbitals, pltpu.HBM),
+    )
+    mine = from_behind(mine, "orb", 1)
     behind = from_behind(here, "orb", 1)
-    lists = block_lists(mine, members)
+    lists = lax.psum(mine, "grp")
     slots = 2 * PAIRS
     fields = jax.ShapeDtypeStruct((members, slots, 2, rows, CELLS), F32)
     packed = pl.pallas_call(
-        pack_kernel,
+        pack_here_kernel,
+        out_shape=fields,
+        in_specs=[smem, vmem],
+        out_specs=vmem,
+        compiler_params=limit,
+        cost_estimate=pl.CostEstimate(flops=10**10, bytes_accessed=1 << 20, transcendentals=0),
+        name="pack_here",
+    )(lists, here)
+    packed = pl.pallas_call(
+        pack_behind_kernel,
         out_shape=fields,
         in_specs=[smem, vmem, vmem],
         out_specs=vmem,
-        compiler_params=limit,
-        name="pack",
-    )(lists, behind, here)
+        input_output_aliases={2: 0},
+        compiler_params=limit,
+        name="pack_behind",
+    )(lists, behind, packed)
     got = lax.all_to_all(packed, "grp", 0, 0)
     tables = [jnp.asarray(table) for table in TABLES]
     buf = pltpu.VMEM((2, SLABS + 2 * PAD_SLABS, BOX + 2 * PAD_ROWS, LANES), F32)
@@ -284,7 +361,7 @@
         scratch_shapes=[buf] * PAIRS,
         compiler_params=limit,
         name="pairs",
-    )(box_offsets, mine, got, *tables)
+    )(box_offsets, lists, got, *tables)
     returned = lax.all_to_all(terms, "grp", 0, 0)
     shape = jax.ShapeDtypeStruct(orbitals.shape, F32)
     back_terms = pl.pallas_call(

time: 69.9 us -> 65.9 us (0.943)
  waiting for transfers between devices: 17 us -> 13.5 us
    ppermute x3, waiting for transfers between devices: 17 us -> 13.5 us  [from_behind(): return lax.ppermute(value, axis, pairs)]
    pallas_call x2 -> x3, Pallas kernels: 1.79 us -> 3.03 us  [the longest x1 1.55 us: local(): pl.pallas_call(entry_kernel, out_shape=(jax.ShapeDtypeStruct((members, 1,...]
    pallas_call x1, Pallas kernels: 3.5 us -> 2.67 us  [local(): pl.pallas_call(pair_kernel, out_shape=fields, in_specs=[smem] * 2 + [vmem...]
  transfers between devices with their start and end apart: 3 -> 3, of which waited for: 2 -> 2; matrix products, arithmetic and copies ran while one was open for 0% -> 0% of each run, Pallas kernels for 1% -> 2%
where the time goes in v3:
time: 65.9 us; the launch traced here: 65.6 us
  blocking collectives  35.7 us (54%)
  waiting for transfers between devices  13.5 us (20%)
  starting transfers between devices  7.43 us (11%)
  Pallas kernels  7.25 us (11%)
  between operations  0.87 us (1%)
  other arithmetic  0.79 us (1%)
    all_to_all x1, blocking collectives, local(): got = lax.all_to_all(packed, 'grp', 0, 0)  14.3 us
    ppermute x3, waiting for transfers between devices, from_behind(): return lax.ppermute(value, axis, pairs)  13.5 us
    all_to_all x1, blocking collectives, local(): returned = lax.all_to_all(terms, 'grp', 0, 0)  13.3 us
    psum x1, blocking collectives, local(): lists = lax.psum(mine, 'grp')  8.01 us
    ppermute x3, starting transfers between devices, from_behind(): return lax.ppermute(value, axis, pairs)  7.43 us
    pallas_call x1, Pallas kernels, local(): pl.pallas_call(pair_kernel, out_shape=fields, in_specs=[smem] * 2 + [vmem...  2.67 us
    pallas_call x1, Pallas kernels, local(): pl.pallas_call(entry_kernel, out_shape=(jax.ShapeDtypeStruct((members, 1,...  1.55 us
  transfers between devices with their start and end apart: 3, of which 2 were waited for; matrix products, arithmetic and copies ran while one was open for 0% of the time, Pallas kernels for 2%

profile of v3, /device:TPU:2, one launch (start us, length us, event | category | flops | bytes accessed | tf_op | source)
XLA Modules:
  0.0 65.6 jit_solution(17842493229019653194)
XLA Ops:
  0.0 0.0 copy-start.8
  0.0 0.0 copy-start.7
  0.7 0.0 copy-done.8
  0.7 0.0 copy-done.7
  0.7 1.5 %entry.1 = (s32[4,1,128]{2,1,0:T(1,128)S(1)}, f32[6,2,8,1024]{3,2,1,0:T(8,128)S(1)}) custom-call(s32[1,1,2]{2,1,0:T(1,128)S(1)} %copy-done.7, s32[1,1,2]{2,1,0:T(1,128)S(1)} %copy-done.8, s32[1,1]{1,0:T(1,128)S(6)} %copy.14.count, f32[6,2,8,1024]{3,2,1,0:T(8,128)} %rows.1), custom_call_target="tpu_custom_call" | custom-call | tf_op jit(solution)/shard_map/entry/pallas_call | solution.py:313
  2.3 1.9 %collective-permute-start = (s32[4,1,128]{2,1,0:T(1,128)S(1)}, s32[4,1,128]{2,1,0:T(1,128)S(1)}, u32[]{:S(2)}, u32[]{:S(2)}) collective-permute-start(s32[4,1,128]{2,1,0:T(1,128)S(1)} %get-tuple-element.7), channel_id=1, source_target_pairs={{0,4},{4,8},{8,12},{12,16},{16,20},{20,24},{24,28},{28,32},{32,36}... | collective-permute-start | bytes 6152 | tf_op jit(solution)/shard_map/ppermute | solution.py:65
  4.2 3.6 %collective-permute-start.1 = (f32[6,2,8,1024]{3,2,1,0:T(8,128)S(1)}, f32[6,2,8,1024]{3,2,1,0:T(8,128)S(1)}, u32[]{:S(2)}, u32[]{:S(2)}) collective-permute-start(f32[6,2,8,1024]{3,2,1,0:T(8,128)S(1)} %get-tuple-element.8.here), channel_id=1, source_target_pairs={{0,4},{4,8},{8,12},{12,16},{16,20},{20,24},{24,28},{28,32},{32,36}... | collective-permute-start | bytes 1179656 | tf_op jit(solution)/shard_map/ppermute | solution.py:65
  7.8 9.0 %collective-permute-done = s32[4,1,128]{2,1,0:T(1,128)S(1)} collective-permute-done((s32[4,1,128]{2,1,0:T(1,128)S(1)}, s32[4,1,128]{2,1,0:T(1,128)S(1)}, u32[]{:S(2)}, u32[]{:S(2)}) %collective-permute-start) | collective-permute-done | bytes 2080 | tf_op jit(solution)/shard_map/ppermute | solution.py:65
  16.8 8.0 %psum.7.lists = s32[4,1,128]{2,1,0:T(1,128)S(1)} all-reduce(s32[4,1,128]{2,1,0:T(1,128)S(1)} %collective-permute-done), channel_id=1, replica_groups=mesh['orb'=128,'grp'=4] {'grp'}, use_global_device_ids=true, to_apply=%region_0.0 | all-reduce | flops 512 | bytes 4096 | tf_op jit(solution)/shard_map/psum | solution.py:332
  24.8 0.7 %pack_here.1.packed = f32[4,4,2,8,1024]{4,3,2,1,0:T(8,128)S(1)} custom-call(s32[4,1,128]{2,1,0:T(1,128)S(1)} %psum.7.lists, f32[6,2,8,1024]{3,2,1,0:T(8,128)S(1)} %get-tuple-element.8.here), custom_call_target="tpu_custom_call" | custom-call | flops 10000000000 | bytes 1048576 | tf_op jit(solution)/shard_map/pack_here/pallas_call | solution.py:335
  25.6 0.0 collective-permute-done.1.behind
  25.6 0.7 %pack_behind.1 = f32[4,4,2,8,1024]{4,3,2,1,0:T(8,128)S(1)} custom-call(s32[4,1,128]{2,1,0:T(1,128)S(1)} %psum.7.lists, f32[6,2,8,1024]{3,2,1,0:T(8,128)S(1)} %collective-permute-done.1.behind, f32[4,4,2,8,1024]{4,3,2,1,0:T(8,128)S(1)} %pack_here.1.packed), custom_call_target="tpu_custom_call", output_to_operand_aliasing={{}: (2, {})} | custom-call | tf_op jit(solution)/shard_map/pack_behind/pallas_call | solution.py:344
  26.3 0.0 copy-start
  26.3 0.0 copy-start.1
  26.4 0.0 copy-start.2
  26.4 0.0 copy-start.3
  26.4 0.0 copy-start.4
  26.4 0.0 copy-start.5
  26.4 0.0 copy-start.6
  26.4 14.3 %all_to_all.10.got = f32[4,4,2,8,1024]{4,3,2,1,0:T(8,128)S(1)} all-to-all(f32[4,4,2,8,1024]{4,3,2,1,0:T(8,128)S(1)} %pack_behind.1), channel_id=1, replica_groups=mesh['orb'=128,'grp'=4] {'grp'}, dimensions={0} | all-to-all | bytes 2097152 | tf_op jit(solution)/shard_map/all_to_all | solution.py:353
  40.8 0.0 copy-done
  40.8 0.0 copy-done.1
  40.8 0.0 copy-done.2
  40.8 0.0 copy-done.3
  40.8 0.0 copy-done.4
  40.8 0.0 copy-done.5
  40.8 0.0 copy-done.6
  40.8 2.7 %pairs.1 = f32[4,4,2,8,1024]{4,3,2,1,0:T(8,128)S(1)} custom-call(s32[3,768]{1,0:T(4,128)S(1)} %copy-done.4, s32[4,1,128]{2,1,0:T(1,128)S(1)} %psum.7.lists, f32[4,4,2,8,1024]{4,3,2,1,0:T(8,128)S(1)} %all_to_all.10.got, bf16[64,96]{1,0:T(8,128)(2,1)S(1)} %copy-done.3, bf16[768,256]{1,0:T(8,128)(2,1)S(1)} %copy-done.1, bf16[768,256]{1,0:T(8,128)(2,1)S(1)} %copy-done, ...), custom_call_target="tpu_custom_call" | custom-call | tf_op jit(solution)/shard_map/pairs/pallas_call | solution.py:356
  43.5 13.3 %all_to_all.11.got = f32[4,4,2,8,1024]{4,3,2,1,0:T(8,128)S(1)} all-to-all(f32[4,4,2,8,1024]{4,3,2,1,0:T(8,128)S(1)} %pairs.1), channel_id=1, replica_groups=mesh['orb'=128,'grp'=4] {'grp'}, dimensions={0} | all-to-all | bytes 2097152 | tf_op jit(solution)/shard_map/all_to_all | solution.py:365
  56.8 0.8 %back_terms.1 = f32[6,2,8,1024]{3,2,1,0:T(8,128)S(1)} custom-call(s32[4,1,128]{2,1,0:T(1,128)S(1)} %psum.7.lists, f32[4,4,2,8,1024]{4,3,2,1,0:T(8,128)S(1)} %all_to_all.11.got), custom_call_target="tpu_custom_call" | custom-call | tf_op jit(solution)/shard_map/back_terms/pallas_call | solution.py:367
  57.6 1.9 %collective-permute-start.2 = (f32[6,2,8,1024]{3,2,1,0:T(8,128)S(1)}, f32[6,2,8,1024]{3,2,1,0:T(8,128)S(1)}, u32[]{:S(2)}, u32[]{:S(2)}) collective-permute-start(f32[6,2,8,1024]{3,2,1,0:T(8,128)S(1)} %back_terms.1), channel_id=1, source_target_pairs={{0,508},{4,0},{8,4},{12,8},{16,12},{20,16},{24,20},{28,24},{32,28}... | collective-permute-start | bytes 1179656 | tf_op jit(solution)/shard_map/ppermute | solution.py:65
  59.5 0.8 %here_terms.1 = f32[6,2,8,1024]{3,2,1,0:T(8,128)S(1)} custom-call(s32[4,1,128]{2,1,0:T(1,128)S(1)} %psum.7.lists, f32[4,4,2,8,1024]{4,3,2,1,0:T(8,128)S(1)} %all_to_all.11.got), custom_call_target="tpu_custom_call" | custom-call | tf_op jit(solution)/shard_map/here_terms/pallas_call | solution.py:376
  60.3 4.5 %collective-permute-done.2 = f32[6,2,8,1024]{3,2,1,0:T(8,128)S(1)} collective-permute-done((f32[6,2,8,1024]{3,2,1,0:T(8,128)S(1)}, f32[6,2,8,1024]{3,2,1,0:T(8,128)S(1)}, u32[]{:S(2)}, u32[]{:S(2)}) %collective-permute-start.2) | collective-permute-done | bytes 393248 | tf_op jit(solution)/shard_map/ppermute | solution.py:65
  64.8 0.8 %add.5 = f32[6,2,8,1024]{3,2,1,0:T(8,128)} add(f32[6,2,8,1024]{3,2,1,0:T(8,128)S(1)} %here_terms.1, f32[6,2,8,1024]{3,2,1,0:T(8,128)S(1)} %collective-permute-done.2) | non-fusion elementwise | flops 98304 | bytes 1179648 | tf_op jit(solution)/shard_map/add | solution.py:384
Async XLA Ops:
  0.0 0.7 %copy-start.8 = (s32[1,1,2]{2,1,0:T(1,128)S(1)}, s32[1,1,2]{2,1,0:T(1,128)}, u32[]{:S(2)}) copy-start(s32[1,1,2]{2,1,0:T(1,128)} %seconds.1) | copy-start | bytes 28
  0.0 0.7 %copy-start.7 = (s32[1,1,2]{2,1,0:T(1,128)S(1)}, s32[1,1,2]{2,1,0:T(1,128)}, u32[]{:S(2)}) copy-start(s32[1,1,2]{2,1,0:T(1,128)} %firsts.1) | copy-start | bytes 28
  2.3 14.6 %collective-permute-start = (s32[4,1,128]{2,1,0:T(1,128)S(1)}, s32[4,1,128]{2,1,0:T(1,128)S(1)}, u32[]{:S(2)}, u32[]{:S(2)}) collective-permute-start(s32[4,1,128]{2,1,0:T(1,128)S(1)} %get-tuple-element.7), channel_id=1, source_target_pairs={{0,4},{4,8},{8,12},{12,16},{16,20},{20,24},{24,28},{28,32},{32,36}... | collective-permute-start | bytes 6152 | tf_op jit(solution)/shard_map/ppermute | solution.py:65
  4.2 21.4 %collective-permute-start.1 = (f32[6,2,8,1024]{3,2,1,0:T(8,128)S(1)}, f32[6,2,8,1024]{3,2,1,0:T(8,128)S(1)}, u32[]{:S(2)}, u32[]{:S(2)}) collective-permute-start(f32[6,2,8,1024]{3,2,1,0:T(8,128)S(1)} %get-tuple-element.8.here), channel_id=1, source_target_pairs={{0,4},{4,8},{8,12},{12,16},{16,20},{20,24},{24,28},{28,32},{32,36}... | collective-permute-start | bytes 1179656 | tf_op jit(solution)/shard_map/ppermute | solution.py:65
  26.3 14.4 %copy-start = (bf16[768,256]{1,0:T(8,128)(2,1)S(1)}, bf16[768,256]{1,0:T(8,128)(2,1)}, u32[]{:S(2)}) copy-start(bf16[768,256]{1,0:T(8,128)(2,1)} %constant.14.clone.back3) | copy-start | bytes 1179652
  26.3 14.4 %copy-start.1 = (bf16[768,256]{1,0:T(8,128)(2,1)S(1)}, bf16[768,256]{1,0:T(8,128)(2,1)}, u32[]{:S(2)}) copy-start(bf16[768,256]{1,0:T(8,128)(2,1)} %constant.13.clone.for3) | copy-start | bytes 1179652
  26.4 14.4 %copy-start.2 = (f32[256,128]{1,0:T(8,128)S(1)}, f32[256,128]{1,0:T(8,128)}, u32[]{:S(2)}) copy-start(f32[256,128]{1,0:T(8,128)} %constant.17.clone.green) | copy-start | bytes 393220
  26.4 14.4 %copy-start.3 = (bf16[64,96]{1,0:T(8,128)(2,1)S(1)}, bf16[64,96]{1,0:T(8,128)(2,1)}, u32[]{:S(2)}) copy-start(bf16[64,96]{1,0:T(8,128)(2,1)} %constant.12.clone.left3) | copy-start | bytes 36868
  26.4 14.4 %copy-start.4 = (s32[3,768]{1,0:T(4,128)S(1)}, s32[3,768]{1,0:T(4,128)}, u32[]{:S(2)}) copy-start(s32[3,768]{1,0:T(4,128)} %offsets.1) | copy-start | bytes 27652
  26.4 14.4 %copy-start.5 = (f32[8,128]{1,0:T(8,128)S(1)}, f32[8,128]{1,0:T(8,128)}, u32[]{:S(2)}) copy-start(f32[8,128]{1,0:T(8,128)} %constant.16.clone.twid_im) | copy-start | bytes 12292
  26.4 14.4 %copy-start.6 = (f32[8,128]{1,0:T(8,128)S(1)}, f32[8,128]{1,0:T(8,128)}, u32[]{:S(2)}) copy-start(f32[8,128]{1,0:T(8,128)} %constant.15.clone.twid_re) | copy-start | bytes 12292
  57.6 7.2 %collective-permute-start.2 = (f32[6,2,8,1024]{3,2,1,0:T(8,128)S(1)}, f32[6,2,8,1024]{3,2,1,0:T(8,128)S(1)}, u32[]{:S(2)}, u32[]{:S(2)}) collective-permute-start(f32[6,2,8,1024]{3,2,1,0:T(8,128)S(1)} %back_terms.1), channel_id=1, source_target_pairs={{0,508},{4,0},{8,4},{12,8},{16,12},{20,16},{24,20},{28,24},{32,28}... | collective-permute-start | bytes 1179656 | tf_op jit(solution)/shard_map/ppermute | solution.py:65

commit v4 on v3

--- a/solution.py
+++ b/solution.py
@@ -72,9 +72,7 @@
     return first % ORB_DEV, second % ORB_DEV, ahead, first != second
 
 
-def entry_kernel(firsts, seconds, count, rows, table, here, sem):
-    copy = pltpu.make_async_copy(rows, here, sem)
-    copy.start()
+def entry_kernel(firsts, seconds, count, table):
     who = lax.broadcasted_iota(jnp.int32, table.shape, 0)
     lane = lax.broadcasted_iota(jnp.int32, table.shape, 2)
     value = jnp.where(lane == 2 * PAIRS, count[0, 0], 0)
@@ -82,25 +80,21 @@
         value = jnp.where(lane == turn, firsts[0, 0, turn], value)
         value = jnp.where(lane == PAIRS + turn, seconds[0, 0, turn], value)
     table[...] = jnp.where(who == lax.axis_index("grp"), value, 0)
-    copy.wait()
-
-
-def pack_here_kernel(lists, here, send):
-    for who in range(send.shape[0]):
-        for turn in range(PAIRS):
-            _, at_second, is_ahead, _ = places(lists, who, turn)
-
-            @pl.when(is_ahead)
-            def _():
-                send[who, 2 * turn + 1] = here[at_second]
-
-
-def pack_behind_kernel(lists, behind, packed, send):
-    del packed
+
+
+def stage_kernel(source, out):
+    pltpu.sync_copy(source, out)
+
+
+def pack_kernel(lists, behind, here, send):
     for who in range(send.shape[0]):
         for turn in range(PAIRS):
             at_first, at_second, is_ahead, _ = places(lists, who, turn)
             send[who, 2 * turn] = behind[at_first]
+
+            @pl.when(is_ahead)
+            def _():
+                send[who, 2 * turn + 1] = here[at_second]
 
             @pl.when(jnp.logical_not(is_ahead))
             def _():
@@ -310,46 +304,37 @@
     vmem = pl.BlockSpec(memory_space=pltpu.VMEM)
     anywhere = pl.BlockSpec(memory_space=pl.ANY)
     limit = pltpu.CompilerParams(vmem_limit_bytes=40 * 1024 * 1024)
-    mine, here = pl.pallas_call(
+    hbm = pl.BlockSpec(memory_space=pltpu.HBM)
+    mine = pl.pallas_call(
         entry_kernel,
-        out_shape=(
-            jax.ShapeDtypeStruct((members, 1, LANES), jnp.int32),
-            jax.ShapeDtypeStruct(orbitals.shape, F32),
-        ),
-        in_specs=[smem] * 3 + [pl.BlockSpec(memory_space=pltpu.HBM)],
-        out_specs=(vmem, vmem),
-        scratch_shapes=[pltpu.SemaphoreType.DMA],
+        out_shape=jax.ShapeDtypeStruct((members, 1, LANES), jnp.int32),
+        in_specs=[smem] * 3,
+        out_specs=vmem,
         compiler_params=limit,
         name="entry",
-    )(
-        pair_first,
-        pair_second,
-        pair_count,
-        pltpu.with_memory_space_constraint(orbitals, pltpu.HBM),
-    )
+    )(pair_first, pair_second, pair_count)
     mine = from_behind(mine, "orb", 1)
-    behind = from_behind(here, "orb", 1)
+    behind = from_behind(orbitals, "orb", 1)
     lists = lax.psum(mine, "grp")
     slots = 2 * PAIRS
     fields = jax.ShapeDtypeStruct((members, slots, 2, rows, CELLS), F32)
+    here = pl.pallas_call(
+        stage_kernel,
+        out_shape=jax.ShapeDtypeStruct(orbitals.shape, F32),
+        in_specs=[hbm],
+        out_specs=vmem,
+        compiler_params=limit,
+        cost_estimate=pl.CostEstimate(flops=10**10, bytes_accessed=1 << 20, transcendentals=0),
+        name="stage",
+    )(pltpu.with_memory_space_constraint(orbitals, pltpu.HBM))
     packed = pl.pallas_call(
-        pack_here_kernel,
-        out_shape=fields,
-        in_specs=[smem, vmem],
-        out_specs=vmem,
-        compiler_params=limit,
-        cost_estimate=pl.CostEstimate(flops=10**10, bytes_accessed=1 << 20, transcendentals=0),
-        name="pack_here",
-    )(lists, here)
-    packed = pl.pallas_call(
-        pack_behind_kernel,
+        pack_kernel,
         out_shape=fields,
         in_specs=[smem, vmem, vmem],
         out_specs=vmem,
-        input_output_aliases={2: 0},
-        compiler_params=limit,
-        name="pack_behind",
-    )(lists, behind, packed)
+        compiler_params=limit,
+        name="pack",
+    )(lists, behind, here)
     got = lax.all_to_all(packed, "grp", 0, 0)
     tables = [jnp.asarray(table) for table in TABLES]
     buf = pltpu.VMEM((2, SLABS + 2 * PAD_SLABS, BOX + 2 * PAD_ROWS, LANES), F32)

time: 65.9 us -> 65.6 us (level)
  starting transfers between devices: 7.43 us -> 8.72 us
  waiting for transfers between devices: 13.5 us -> 12.5 us
  Pallas kernels: 7.25 us -> 6.57 us
    ppermute x3, starting transfers between devices: 7.43 us -> 8.72 us  [from_behind(): return lax.ppermute(value, axis, pairs)]
    ppermute x3, waiting for transfers between devices: 13.5 us -> 12.5 us  [from_behind(): return lax.ppermute(value, axis, pairs)]
    pallas_call x3, Pallas kernels: 3.03 us -> 2.35 us  [the longest x1 1 us: local(): pl.pallas_call(stage_kernel, out_shape=jax.ShapeDtypeStruct(orbitals.shap...]
  transfers between devices with their start and end apart: 3 -> 3, of which waited for: 2 -> 2; matrix products, arithmetic and copies ran while one was open for 0% -> 0% of each run, Pallas kernels for 2% -> 3%
where the time goes in v4:
time: 65.6 us; the launch traced here: 65.3 us
  blocking collectives  35.8 us (55%)
  waiting for transfers between devices  12.5 us (19%)
  starting transfers between devices  8.72 us (13%)
  Pallas kernels  6.57 us (10%)
  between operations  0.85 us (1%)
  other arithmetic  0.79 us (1%)
    all_to_all x1, blocking collectives, local(): got = lax.all_to_all(packed, 'grp', 0, 0)  14.4 us
    all_to_all x1, blocking collectives, local(): returned = lax.all_to_all(terms, 'grp', 0, 0)  13.3 us
    ppermute x3, waiting for transfers between devices, from_behind(): return lax.ppermute(value, axis, pairs)  12.5 us
    ppermute x3, starting transfers between devices, from_behind(): return lax.ppermute(value, axis, pairs)  8.72 us
    psum x1, blocking collectives, local(): lists = lax.psum(mine, 'grp')  8.1 us
    pallas_call x1, Pallas kernels, local(): pl.pallas_call(pair_kernel, out_shape=fields, in_specs=[smem] * 2 + [vmem...  2.66 us
  transfers between devices with their start and end apart: 3, of which 2 were waited for; matrix products, arithmetic and copies ran while one was open for 0% of the time, Pallas kernels for 3%

profile of v4, /device:TPU:2, one launch (start us, length us, event | category | flops | bytes accessed | tf_op | source)
XLA Modules:
  0.0 65.3 jit_solution(16215435705672365846)
XLA Ops:
  0.0 0.0 copy-start.8
  0.0 0.0 copy-start.7
  0.7 0.0 copy-done.8
  0.7 0.0 copy-done.7
  0.7 0.6 entry.1
  1.3 1.9 %collective-permute-start = (s32[4,1,128]{2,1,0:T(1,128)S(1)}, s32[4,1,128]{2,1,0:T(1,128)S(1)}, u32[]{:S(2)}, u32[]{:S(2)}) collective-permute-start(s32[4,1,128]{2,1,0:T(1,128)S(1)} %entry.1), channel_id=1, source_target_pairs={{0,4},{4,8},{8,12},{12,16},{16,20},{20,24},{24,28},{28,32},{32,36}... | collective-permute-start | bytes 6152 | tf_op jit(solution)/shard_map/ppermute | solution.py:65
  3.2 3.6 %collective-permute-start.1 = (f32[6,2,8,1024]{3,2,1,0:T(8,128)}, f32[6,2,8,1024]{3,2,1,0:T(8,128)S(1)}, u32[]{:S(2)}, u32[]{:S(2)}) collective-permute-start(f32[6,2,8,1024]{3,2,1,0:T(8,128)} %source.1), channel_id=1, source_target_pairs={{0,4},{4,8},{8,12},{12,16},{16,20},{20,24},{24,28},{28,32},{32,36}... | collective-permute-start | bytes 1179656 | tf_op jit(solution)/shard_map/ppermute | solution.py:65
  6.8 1.0 %stage.1.here = f32[6,2,8,1024]{3,2,1,0:T(8,128)S(1)} custom-call(f32[6,2,8,1024]{3,2,1,0:T(8,128)} %source.1), custom_call_target="tpu_custom_call" | custom-call | flops 10000000000 | bytes 1048576 | tf_op jit(solution)/shard_map/stage/pallas_call | solution.py:321
  7.8 8.0 %collective-permute-done = s32[4,1,128]{2,1,0:T(1,128)S(1)} collective-permute-done((s32[4,1,128]{2,1,0:T(1,128)S(1)}, s32[4,1,128]{2,1,0:T(1,128)S(1)}, u32[]{:S(2)}, u32[]{:S(2)}) %collective-permute-start) | collective-permute-done | bytes 2080 | tf_op jit(solution)/shard_map/ppermute | solution.py:65
  15.8 8.1 %psum.7.lists = s32[4,1,128]{2,1,0:T(1,128)S(1)} all-reduce(s32[4,1,128]{2,1,0:T(1,128)S(1)} %collective-permute-done), channel_id=1, replica_groups=mesh['orb'=128,'grp'=4] {'grp'}, use_global_device_ids=true, to_apply=%region_0.0 | all-reduce | flops 512 | bytes 4096 | tf_op jit(solution)/shard_map/psum | solution.py:318
  23.9 0.0 collective-permute-done.1.behind
  23.9 0.8 %pack.1 = f32[4,4,2,8,1024]{4,3,2,1,0:T(8,128)S(1)} custom-call(s32[4,1,128]{2,1,0:T(1,128)S(1)} %psum.7.lists, f32[6,2,8,1024]{3,2,1,0:T(8,128)S(1)} %collective-permute-done.1.behind, f32[6,2,8,1024]{3,2,1,0:T(8,128)S(1)} %stage.1.here), custom_call_target="tpu_custom_call" | custom-call | tf_op jit(solution)/shard_map/pack/pallas_call | solution.py:330
  24.7 0.0 copy-start
  24.7 0.0 copy-start.1
  24.8 0.0 copy-start.2
  24.8 0.0 copy-start.3
  24.8 0.0 copy-start.4
  24.8 0.0 copy-start.5
  24.8 0.0 copy-start.6
  24.8 14.4 %all_to_all.10.got = f32[4,4,2,8,1024]{4,3,2,1,0:T(8,128)S(1)} all-to-all(f32[4,4,2,8,1024]{4,3,2,1,0:T(8,128)S(1)} %pack.1), channel_id=1, replica_groups=mesh['orb'=128,'grp'=4] {'grp'}, dimensions={0} | all-to-all | bytes 2097152 | tf_op jit(solution)/shard_map/all_to_all | solution.py:338
  39.2 0.0 copy-done
  39.2 0.0 copy-done.1
  39.2 0.0 copy-done.2
  39.2 0.0 copy-done.3
  39.2 0.0 copy-done.4
  39.2 0.0 copy-done.5
  39.2 0.0 copy-done.6
  39.2 2.7 %pairs.1 = f32[4,4,2,8,1024]{4,3,2,1,0:T(8,128)S(1)} custom-call(s32[3,768]{1,0:T(4,128)S(1)} %copy-done.4, s32[4,1,128]{2,1,0:T(1,128)S(1)} %psum.7.lists, f32[4,4,2,8,1024]{4,3,2,1,0:T(8,128)S(1)} %all_to_all.10.got, bf16[64,96]{1,0:T(8,128)(2,1)S(1)} %copy-done.3, bf16[768,256]{1,0:T(8,128)(2,1)S(1)} %copy-done.1, bf16[768,256]{1,0:T(8,128)(2,1)S(1)} %copy-done, ...), custom_call_target="tpu_custom_call" | custom-call | tf_op jit(solution)/shard_map/pairs/pallas_call | solution.py:341
  41.9 13.3 %all_to_all.11.got = f32[4,4,2,8,1024]{4,3,2,1,0:T(8,128)S(1)} all-to-all(f32[4,4,2,8,1024]{4,3,2,1,0:T(8,128)S(1)} %pairs.1), channel_id=1, replica_groups=mesh['orb'=128,'grp'=4] {'grp'}, dimensions={0} | all-to-all | bytes 2097152 | tf_op jit(solution)/shard_map/all_to_all | solution.py:350
  55.2 0.8 %back_terms.1 = f32[6,2,8,1024]{3,2,1,0:T(8,128)S(1)} custom-call(s32[4,1,128]{2,1,0:T(1,128)S(1)} %psum.7.lists, f32[4,4,2,8,1024]{4,3,2,1,0:T(8,128)S(1)} %all_to_all.11.got), custom_call_target="tpu_custom_call" | custom-call | tf_op jit(solution)/shard_map/back_terms/pallas_call | solution.py:352
  56.0 3.2 %collective-permute-start.2 = (f32[6,2,8,1024]{3,2,1,0:T(8,128)S(1)}, f32[6,2,8,1024]{3,2,1,0:T(8,128)S(1)}, u32[]{:S(2)}, u32[]{:S(2)}) collective-permute-start(f32[6,2,8,1024]{3,2,1,0:T(8,128)S(1)} %back_terms.1), channel_id=1, source_target_pairs={{0,508},{4,0},{8,4},{12,8},{16,12},{20,16},{24,20},{28,24},{32,28}... | collective-permute-start | bytes 1179656 | tf_op jit(solution)/shard_map/ppermute | solution.py:65
  59.3 0.7 %here_terms.1 = f32[6,2,8,1024]{3,2,1,0:T(8,128)S(1)} custom-call(s32[4,1,128]{2,1,0:T(1,128)S(1)} %psum.7.lists, f32[4,4,2,8,1024]{4,3,2,1,0:T(8,128)S(1)} %all_to_all.11.got), custom_call_target="tpu_custom_call" | custom-call | tf_op jit(solution)/shard_map/here_terms/pallas_call | solution.py:361
  60.0 4.5 %collective-permute-done.2 = f32[6,2,8,1024]{3,2,1,0:T(8,128)S(1)} collective-permute-done((f32[6,2,8,1024]{3,2,1,0:T(8,128)S(1)}, f32[6,2,8,1024]{3,2,1,0:T(8,128)S(1)}, u32[]{:S(2)}, u32[]{:S(2)}) %collective-permute-start.2) | collective-permute-done | bytes 393248 | tf_op jit(solution)/shard_map/ppermute | solution.py:65
  64.5 0.8 %add.5 = f32[6,2,8,1024]{3,2,1,0:T(8,128)} add(f32[6,2,8,1024]{3,2,1,0:T(8,128)S(1)} %here_terms.1, f32[6,2,8,1024]{3,2,1,0:T(8,128)S(1)} %collective-permute-done.2) | non-fusion elementwise | flops 98304 | bytes 1179648 | tf_op jit(solution)/shard_map/add | solution.py:369
Async XLA Ops:
  0.0 0.7 %copy-start.8 = (s32[1,1,2]{2,1,0:T(1,128)S(1)}, s32[1,1,2]{2,1,0:T(1,128)}, u32[]{:S(2)}) copy-start(s32[1,1,2]{2,1,0:T(1,128)} %seconds.1) | copy-start | bytes 28
  0.0 0.7 %copy-start.7 = (s32[1,1,2]{2,1,0:T(1,128)S(1)}, s32[1,1,2]{2,1,0:T(1,128)}, u32[]{:S(2)}) copy-start(s32[1,1,2]{2,1,0:T(1,128)} %firsts.1) | copy-start | bytes 28
  1.3 14.6 %collective-permute-start = (s32[4,1,128]{2,1,0:T(1,128)S(1)}, s32[4,1,128]{2,1,0:T(1,128)S(1)}, u32[]{:S(2)}, u32[]{:S(2)}) collective-permute-start(s32[4,1,128]{2,1,0:T(1,128)S(1)} %entry.1), channel_id=1, source_target_pairs={{0,4},{4,8},{8,12},{12,16},{16,20},{20,24},{24,28},{28,32},{32,36}... | collective-permute-start | bytes 6152 | tf_op jit(solution)/shard_map/ppermute | solution.py:65
  3.2 20.7 %collective-permute-start.1 = (f32[6,2,8,1024]{3,2,1,0:T(8,128)}, f32[6,2,8,1024]{3,2,1,0:T(8,128)S(1)}, u32[]{:S(2)}, u32[]{:S(2)}) collective-permute-start(f32[6,2,8,1024]{3,2,1,0:T(8,128)} %source.1), channel_id=1, source_target_pairs={{0,4},{4,8},{8,12},{12,16},{16,20},{20,24},{24,28},{28,32},{32,36}... | collective-permute-start | bytes 1179656 | tf_op jit(solution)/shard_map/ppermute | solution.py:65
  24.7 14.4 %copy-start = (bf16[768,256]{1,0:T(8,128)(2,1)S(1)}, bf16[768,256]{1,0:T(8,128)(2,1)}, u32[]{:S(2)}) copy-start(bf16[768,256]{1,0:T(8,128)(2,1)} %constant.14.clone.back3) | copy-start | bytes 1179652
  24.7 14.4 %copy-start.1 = (bf16[768,256]{1,0:T(8,128)(2,1)S(1)}, bf16[768,256]{1,0:T(8,128)(2,1)}, u32[]{:S(2)}) copy-start(bf16[768,256]{1,0:T(8,128)(2,1)} %constant.13.clone.for3) | copy-start | bytes 1179652
  24.8 14.4 %copy-start.2 = (f32[256,128]{1,0:T(8,128)S(1)}, f32[256,128]{1,0:T(8,128)}, u32[]{:S(2)}) copy-start(f32[256,128]{1,0:T(8,128)} %constant.17.clone.green) | copy-start | bytes 393220
  24.8 14.4 %copy-start.3 = (bf16[64,96]{1,0:T(8,128)(2,1)S(1)}, bf16[64,96]{1,0:T(8,128)(2,1)}, u32[]{:S(2)}) copy-start(bf16[64,96]{1,0:T(8,128)(2,1)} %constant.12.clone.left3) | copy-start | bytes 36868
  24.8 14.4 %copy-start.4 = (s32[3,768]{1,0:T(4,128)S(1)}, s32[3,768]{1,0:T(4,128)}, u32[]{:S(2)}) copy-start(s32[3,768]{1,0:T(4,128)} %offsets.1) | copy-start | bytes 27652
  24.8 14.4 %copy-start.5 = (f32[8,128]{1,0:T(8,128)S(1)}, f32[8,128]{1,0:T(8,128)}, u32[]{:S(2)}) copy-start(f32[8,128]{1,0:T(8,128)} %constant.16.clone.twid_im) | copy-start | bytes 12292
  24.8 14.4 %copy-start.6 = (f32[8,128]{1,0:T(8,128)S(1)}, f32[8,128]{1,0:T(8,128)}, u32[]{:S(2)}) copy-start(f32[8,128]{1,0:T(8,128)} %constant.15.clone.twid_re) | copy-start | bytes 12292
  56.0 8.5 %collective-permute-start.2 = (f32[6,2,8,1024]{3,2,1,0:T(8,128)S(1)}, f32[6,2,8,1024]{3,2,1,0:T(8,128)S(1)}, u32[]{:S(2)}, u32[]{:S(2)}) collective-permute-start(f32[6,2,8,1024]{3,2,1,0:T(8,128)S(1)} %back_terms.1), channel_id=1, source_target_pairs={{0,508},{4,0},{8,4},{12,8},{16,12},{20,16},{24,20},{28,24},{32,28}... | collective-permute-start | bytes 1179656 | tf_op jit(solution)/shard_map/ppermute | solution.py:65

commit v5 on v4

--- a/solution.py
+++ b/solution.py
@@ -75,10 +75,14 @@
 def entry_kernel(firsts, seconds, count, table):
     who = lax.broadcasted_iota(jnp.int32, table.shape, 0)
     lane = lax.broadcasted_iota(jnp.int32, table.shape, 2)
-    value = jnp.where(lane == 2 * PAIRS, count[0, 0], 0)
+
+    def spread(value):
+        return jnp.broadcast_to(value.reshape(1, 1, 1), table.shape)
+
+    value = jnp.where(lane == 2 * PAIRS, spread(count[...]), 0)
     for turn in range(PAIRS):
-        value = jnp.where(lane == turn, firsts[0, 0, turn], value)
-        value = jnp.where(lane == PAIRS + turn, seconds[0, 0, turn], value)
+        value = jnp.where(lane == turn, spread(firsts[:, :, turn : turn + 1]), value)
+        value = jnp.where(lane == PAIRS + turn, spread(seconds[:, :, turn : turn + 1]), value)
     table[...] = jnp.where(who == lax.axis_index("grp"), value, 0)
 
 
@@ -308,7 +312,7 @@
     mine = pl.pallas_call(
         entry_kernel,
         out_shape=jax.ShapeDtypeStruct((members, 1, LANES), jnp.int32),
-        in_specs=[smem] * 3,
+        in_specs=[vmem] * 3,
         out_specs=vmem,
         compiler_params=limit,
         name="entry",

time: 65.6 us -> 65.1 us (level)
  no operation moved by 1% of the time
where the time goes in v5:
time: 65.1 us; the launch traced here: 64.8 us
  blocking collectives  35.8 us (55%)
  waiting for transfers between devices  12.5 us (19%)
  starting transfers between devices  8.7 us (13%)
  Pallas kernels  6.1 us (9%)
  between operations  0.85 us (1%)
  other arithmetic  0.79 us (1%)
    all_to_all x1, blocking collectives, local(): got = lax.all_to_all(packed, 'grp', 0, 0)  14.4 us
    all_to_all x1, blocking collectives, local(): returned = lax.all_to_all(terms, 'grp', 0, 0)  13.3 us
    ppermute x3, waiting for transfers between devices, from_behind(): return lax.ppermute(value, axis, pairs)  12.5 us
    ppermute x3, starting transfers between devices, from_behind(): return lax.ppermute(value, axis, pairs)  8.7 us
    psum x1, blocking collectives, local(): lists = lax.psum(mine, 'grp')  8.1 us
    pallas_call x1, Pallas kernels, local(): pl.pallas_call(pair_kernel, out_shape=fields, in_specs=[smem] * 2 + [vmem...  2.67 us
  transfers between devices with their start and end apart: 3, of which 2 were waited for; matrix products, arithmetic and copies ran while one was open for 0% of the time, Pallas kernels for 3%

profile of v5, /device:TPU:2, one launch (start us, length us, event | category | flops | bytes accessed | tf_op | source)
XLA Modules:
  0.0 64.8 jit_solution(7394500789183069727)
XLA Ops:
  0.0 0.0 copy-start.8
  0.0 0.0 copy-start.7
  0.7 0.0 copy-done.8
  0.7 0.0 copy-done.7
  0.7 0.1 entry.1
  0.8 1.9 %collective-permute-start = (s32[4,1,128]{2,1,0:T(1,128)S(1)}, s32[4,1,128]{2,1,0:T(1,128)S(1)}, u32[]{:S(2)}, u32[]{:S(2)}) collective-permute-start(s32[4,1,128]{2,1,0:T(1,128)S(1)} %entry.1), channel_id=1, source_target_pairs={{0,4},{4,8},{8,12},{12,16},{16,20},{20,24},{24,28},{28,32},{32,36}... | collective-permute-start | bytes 6152 | tf_op jit(solution)/shard_map/ppermute | solution.py:65
  2.7 3.6 %collective-permute-start.1 = (f32[6,2,8,1024]{3,2,1,0:T(8,128)}, f32[6,2,8,1024]{3,2,1,0:T(8,128)S(1)}, u32[]{:S(2)}, u32[]{:S(2)}) collective-permute-start(f32[6,2,8,1024]{3,2,1,0:T(8,128)} %source.1), channel_id=1, source_target_pairs={{0,4},{4,8},{8,12},{12,16},{16,20},{20,24},{24,28},{28,32},{32,36}... | collective-permute-start | bytes 1179656 | tf_op jit(solution)/shard_map/ppermute | solution.py:65
  6.3 1.0 %stage.1.here = f32[6,2,8,1024]{3,2,1,0:T(8,128)S(1)} custom-call(f32[6,2,8,1024]{3,2,1,0:T(8,128)} %source.1), custom_call_target="tpu_custom_call" | custom-call | flops 10000000000 | bytes 1048576 | tf_op jit(solution)/shard_map/stage/pallas_call | solution.py:325
  7.3 8.0 %collective-permute-done = s32[4,1,128]{2,1,0:T(1,128)S(1)} collective-permute-done((s32[4,1,128]{2,1,0:T(1,128)S(1)}, s32[4,1,128]{2,1,0:T(1,128)S(1)}, u32[]{:S(2)}, u32[]{:S(2)}) %collective-permute-start) | collective-permute-done | bytes 2080 | tf_op jit(solution)/shard_map/ppermute | solution.py:65
  15.3 8.1 %psum.7.lists = s32[4,1,128]{2,1,0:T(1,128)S(1)} all-reduce(s32[4,1,128]{2,1,0:T(1,128)S(1)} %collective-permute-done), channel_id=1, replica_groups=mesh['orb'=128,'grp'=4] {'grp'}, use_global_device_ids=true, to_apply=%region_0.0 | all-reduce | flops 512 | bytes 4096 | tf_op jit(solution)/shard_map/psum | solution.py:322
  23.4 0.0 collective-permute-done.1.behind
  23.4 0.8 %pack.1 = f32[4,4,2,8,1024]{4,3,2,1,0:T(8,128)S(1)} custom-call(s32[4,1,128]{2,1,0:T(1,128)S(1)} %psum.7.lists, f32[6,2,8,1024]{3,2,1,0:T(8,128)S(1)} %collective-permute-done.1.behind, f32[6,2,8,1024]{3,2,1,0:T(8,128)S(1)} %stage.1.here), custom_call_target="tpu_custom_call" | custom-call | tf_op jit(solution)/shard_map/pack/pallas_call | solution.py:334
  24.2 0.0 copy-start
  24.2 0.0 copy-start.1
  24.3 0.0 copy-start.2
  24.3 0.0 copy-start.3
  24.3 0.0 copy-start.4
  24.3 0.0 copy-start.5
  24.3 0.0 copy-start.6
  24.3 14.4 %all_to_all.10.got = f32[4,4,2,8,1024]{4,3,2,1,0:T(8,128)S(1)} all-to-all(f32[4,4,2,8,1024]{4,3,2,1,0:T(8,128)S(1)} %pack.1), channel_id=1, replica_groups=mesh['orb'=128,'grp'=4] {'grp'}, dimensions={0} | all-to-all | bytes 2097152 | tf_op jit(solution)/shard_map/all_to_all | solution.py:342
  38.7 0.0 copy-done
  38.7 0.0 copy-done.1
  38.7 0.0 copy-done.2
  38.7 0.0 copy-done.3
  38.7 0.0 copy-done.4
  38.7 0.0 copy-done.5
  38.7 0.0 copy-done.6
  38.7 2.7 %pairs.1 = f32[4,4,2,8,1024]{4,3,2,1,0:T(8,128)S(1)} custom-call(s32[3,768]{1,0:T(4,128)S(1)} %copy-done.4, s32[4,1,128]{2,1,0:T(1,128)S(1)} %psum.7.lists, f32[4,4,2,8,1024]{4,3,2,1,0:T(8,128)S(1)} %all_to_all.10.got, bf16[64,96]{1,0:T(8,128)(2,1)S(1)} %copy-done.3, bf16[768,256]{1,0:T(8,128)(2,1)S(1)} %copy-done.1, bf16[768,256]{1,0:T(8,128)(2,1)S(1)} %copy-done, ...), custom_call_target="tpu_custom_call" | custom-call | tf_op jit(solution)/shard_map/pairs/pallas_call | solution.py:345
  41.4 13.3 %all_to_all.11.got = f32[4,4,2,8,1024]{4,3,2,1,0:T(8,128)S(1)} all-to-all(f32[4,4,2,8,1024]{4,3,2,1,0:T(8,128)S(1)} %pairs.1), channel_id=1, replica_groups=mesh['orb'=128,'grp'=4] {'grp'}, dimensions={0} | all-to-all | bytes 2097152 | tf_op jit(solution)/shard_map/all_to_all | solution.py:354
  54.7 0.8 %back_terms.1 = f32[6,2,8,1024]{3,2,1,0:T(8,128)S(1)} custom-call(s32[4,1,128]{2,1,0:T(1,128)S(1)} %psum.7.lists, f32[4,4,2,8,1024]{4,3,2,1,0:T(8,128)S(1)} %all_to_all.11.got), custom_call_target="tpu_custom_call" | custom-call | tf_op jit(solution)/shard_map/back_terms/pallas_call | solution.py:356
  55.5 3.2 %collective-permute-start.2 = (f32[6,2,8,1024]{3,2,1,0:T(8,128)S(1)}, f32[6,2,8,1024]{3,2,1,0:T(8,128)S(1)}, u32[]{:S(2)}, u32[]{:S(2)}) collective-permute-start(f32[6,2,8,1024]{3,2,1,0:T(8,128)S(1)} %back_terms.1), channel_id=1, source_target_pairs={{0,508},{4,0},{8,4},{12,8},{16,12},{20,16},{24,20},{28,24},{32,28}... | collective-permute-start | bytes 1179656 | tf_op jit(solution)/shard_map/ppermute | solution.py:65
  58.8 0.8 %here_terms.1 = f32[6,2,8,1024]{3,2,1,0:T(8,128)S(1)} custom-call(s32[4,1,128]{2,1,0:T(1,128)S(1)} %psum.7.lists, f32[4,4,2,8,1024]{4,3,2,1,0:T(8,128)S(1)} %all_to_all.11.got), custom_call_target="tpu_custom_call" | custom-call | tf_op jit(solution)/shard_map/here_terms/pallas_call | solution.py:365
  59.5 4.5 %collective-permute-done.2 = f32[6,2,8,1024]{3,2,1,0:T(8,128)S(1)} collective-permute-done((f32[6,2,8,1024]{3,2,1,0:T(8,128)S(1)}, f32[6,2,8,1024]{3,2,1,0:T(8,128)S(1)}, u32[]{:S(2)}, u32[]{:S(2)}) %collective-permute-start.2) | collective-permute-done | bytes 393248 | tf_op jit(solution)/shard_map/ppermute | solution.py:65
  64.0 0.8 %add.5 = f32[6,2,8,1024]{3,2,1,0:T(8,128)} add(f32[6,2,8,1024]{3,2,1,0:T(8,128)S(1)} %here_terms.1, f32[6,2,8,1024]{3,2,1,0:T(8,128)S(1)} %collective-permute-done.2) | non-fusion elementwise | flops 98304 | bytes 1179648 | tf_op jit(solution)/shard_map/add | solution.py:373
Async XLA Ops:
  0.0 0.7 %copy-start.8 = (s32[1,1,2]{2,1,0:T(1,128)S(1)}, s32[1,1,2]{2,1,0:T(1,128)}, u32[]{:S(2)}) copy-start(s32[1,1,2]{2,1,0:T(1,128)} %seconds.1) | copy-start | bytes 28
  0.0 0.7 %copy-start.7 = (s32[1,1,2]{2,1,0:T(1,128)S(1)}, s32[1,1,2]{2,1,0:T(1,128)}, u32[]{:S(2)}) copy-start(s32[1,1,2]{2,1,0:T(1,128)} %firsts.1) | copy-start | bytes 28
  0.8 14.5 %collective-permute-start = (s32[4,1,128]{2,1,0:T(1,128)S(1)}, s32[4,1,128]{2,1,0:T(1,128)S(1)}, u32[]{:S(2)}, u32[]{:S(2)}) collective-permute-start(s32[4,1,128]{2,1,0:T(1,128)S(1)} %entry.1), channel_id=1, source_target_pairs={{0,4},{4,8},{8,12},{12,16},{16,20},{20,24},{24,28},{28,32},{32,36}... | collective-permute-start | bytes 6152 | tf_op jit(solution)/shard_map/ppermute | solution.py:65
  2.7 20.7 %collective-permute-start.1 = (f32[6,2,8,1024]{3,2,1,0:T(8,128)}, f32[6,2,8,1024]{3,2,1,0:T(8,128)S(1)}, u32[]{:S(2)}, u32[]{:S(2)}) collective-permute-start(f32[6,2,8,1024]{3,2,1,0:T(8,128)} %source.1), channel_id=1, source_target_pairs={{0,4},{4,8},{8,12},{12,16},{16,20},{20,24},{24,28},{28,32},{32,36}... | collective-permute-start | bytes 1179656 | tf_op jit(solution)/shard_map/ppermute | solution.py:65
  24.2 14.5 %copy-start = (bf16[768,256]{1,0:T(8,128)(2,1)S(1)}, bf16[768,256]{1,0:T(8,128)(2,1)}, u32[]{:S(2)}) copy-start(bf16[768,256]{1,0:T(8,128)(2,1)} %constant.14.clone.back3) | copy-start | bytes 1179652
  24.2 14.5 %copy-start.1 = (bf16[768,256]{1,0:T(8,128)(2,1)S(1)}, bf16[768,256]{1,0:T(8,128)(2,1)}, u32[]{:S(2)}) copy-start(bf16[768,256]{1,0:T(8,128)(2,1)} %constant.13.clone.for3) | copy-start | bytes 1179652
  24.3 14.4 %copy-start.2 = (f32[256,128]{1,0:T(8,128)S(1)}, f32[256,128]{1,0:T(8,128)}, u32[]{:S(2)}) copy-start(f32[256,128]{1,0:T(8,128)} %constant.17.clone.green) | copy-start | bytes 393220
  24.3 14.4 %copy-start.3 = (bf16[64,96]{1,0:T(8,128)(2,1)S(1)}, bf16[64,96]{1,0:T(8,128)(2,1)}, u32[]{:S(2)}) copy-start(bf16[64,96]{1,0:T(8,128)(2,1)} %constant.12.clone.left3) | copy-start | bytes 36868
  24.3 14.4 %copy-start.4 = (s32[3,768]{1,0:T(4,128)S(1)}, s32[3,768]{1,0:T(4,128)}, u32[]{:S(2)}) copy-start(s32[3,768]{1,0:T(4,128)} %offsets.1) | copy-start | bytes 27652
  24.3 14.4 %copy-start.5 = (f32[8,128]{1,0:T(8,128)S(1)}, f32[8,128]{1,0:T(8,128)}, u32[]{:S(2)}) copy-start(f32[8,128]{1,0:T(8,128)} %constant.16.clone.twid_im) | copy-start | bytes 12292
  24.3 14.4 %copy-start.6 = (f32[8,128]{1,0:T(8,128)S(1)}, f32[8,128]{1,0:T(8,128)}, u32[]{:S(2)}) copy-start(f32[8,128]{1,0:T(8,128)} %constant.15.clone.twid_re) | copy-start | bytes 12292
  55.5 8.5 %collective-permute-start.2 = (f32[6,2,8,1024]{3,2,1,0:T(8,128)S(1)}, f32[6,2,8,1024]{3,2,1,0:T(8,128)S(1)}, u32[]{:S(2)}, u32[]{:S(2)}) collective-permute-start(f32[6,2,8,1024]{3,2,1,0:T(8,128)S(1)} %back_terms.1), channel_id=1, source_target_pairs={{0,508},{4,0},{8,4},{12,8},{16,12},{20,16},{24,20},{28,24},{32,28}... | collective-permute-start | bytes 1179656 | tf_op jit(solution)/shard_map/ppermute | solution.py:65

commit v6 on v5

--- a/solution.py
+++ b/solution.py
@@ -65,13 +65,6 @@
     return lax.ppermute(value, axis, pairs)
 
 
-def places(lists, who, turn):
-    first = lists[who, 0, turn]
-    second = lists[who, 0, PAIRS + turn]
-    ahead = (first // ORB_DEV) != (second // ORB_DEV)
-    return first % ORB_DEV, second % ORB_DEV, ahead, first != second
-
-
 def entry_kernel(firsts, seconds, count, table):
     who = lax.broadcasted_iota(jnp.int32, table.shape, 0)
     lane = lax.broadcasted_iota(jnp.int32, table.shape, 2)
@@ -79,11 +72,28 @@
     def spread(value):
         return jnp.broadcast_to(value.reshape(1, 1, 1), table.shape)
 
-    value = jnp.where(lane == 2 * PAIRS, spread(count[...]), 0)
+    def block_of(orbital):
+        return (orbital * 10923) >> 16
+
+    live = spread(count[...])
+    row = jnp.zeros(table.shape, jnp.int32)
     for turn in range(PAIRS):
-        value = jnp.where(lane == turn, spread(firsts[:, :, turn : turn + 1]), value)
-        value = jnp.where(lane == PAIRS + turn, spread(seconds[:, :, turn : turn + 1]), value)
-    table[...] = jnp.where(who == lax.axis_index("grp"), value, 0)
+        first = spread(firsts[:, :, turn : turn + 1])
+        second = spread(seconds[:, :, turn : turn + 1])
+        first_block, second_block = block_of(first), block_of(second)
+        code = (first - first_block * ORB_DEV) | ((second - second_block * ORB_DEV) << 3)
+        code |= jnp.where(first_block != second_block, 64, 0)
+        code |= jnp.where(first != second, 128, 0)
+        code |= jnp.where(turn < live, 256, 0)
+        row = jnp.where(lane == 3 * turn, first, row)
+        row = jnp.where(lane == 3 * turn + 1, second, row)
+        row = jnp.where(lane == 3 * turn + 2, code, row)
+    table[...] = jnp.where(who == lax.axis_index("grp"), row, 0)
+
+
+def places(lists, who, turn):
+    code = lists[who, 0, 3 * turn + 2]
+    return code & 7, (code >> 3) & 7, (code & 64) != 0, (code & 128) != 0, (code & 256) != 0
 
 
 def stage_kernel(source, out):
@@ -93,7 +103,7 @@
 def pack_kernel(lists, behind, here, send):
     for who in range(send.shape[0]):
         for turn in range(PAIRS):
-            at_first, at_second, is_ahead, _ = places(lists, who, turn)
+            at_first, at_second, is_ahead, _, _ = places(lists, who, turn)
             send[who, 2 * turn] = behind[at_first]
 
             @pl.when(is_ahead)
@@ -243,8 +253,8 @@
 
     moves, moved, firsts, rhos = [], [], [], []
     for turn in range(PAIRS):
-        first = lists[me, 0, turn]
-        second = lists[me, 0, PAIRS + turn]
+        first = lists[me, 0, 3 * turn]
+        second = lists[me, 0, 3 * turn + 1]
         move = []
         for axis in range(3):
             gap = offsets[axis, second] - offsets[axis, first] + GRID // 2
@@ -278,9 +288,9 @@
     out[...] = jnp.zeros(out.shape, F32)
     for who in range(got.shape[0]):
         for turn in range(PAIRS):
-            _, at_second, is_ahead, _ = places(lists, who, turn)
-
-            @pl.when(is_ahead & (turn < lists[who, 0, 2 * PAIRS]))
+            _, at_second, is_ahead, _, live = places(lists, who, turn)
+
+            @pl.when(is_ahead & live)
             def _():
                 out[at_second] -= got[who, 2 * turn + 1]
 
@@ -289,8 +299,7 @@
     out[...] = jnp.zeros(out.shape, F32)
     for who in range(got.shape[0]):
         for turn in range(PAIRS):
-            at_first, at_second, is_ahead, differs = places(lists, who, turn)
-            live = turn < lists[who, 0, 2 * PAIRS]
+            at_first, at_second, is_ahead, differs, live = places(lists, who, turn)
 
             @pl.when(live)
             def _():

time: 65.1 us -> 65 us (level)
  no operation moved by 1% of the time
where the time goes in v6:
time: 65 us; the launch traced here: 64.7 us
  blocking collectives  35.8 us (55%)
  waiting for transfers between devices  12.6 us (19%)
  starting transfers between devices  8.72 us (13%)
  Pallas kernels  5.89 us (9%)
  between operations  0.85 us (1%)
  other arithmetic  0.79 us (1%)
    all_to_all x1, blocking collectives, local(): got = lax.all_to_all(packed, 'grp', 0, 0)  14.4 us
    all_to_all x1, blocking collectives, local(): returned = lax.all_to_all(terms, 'grp', 0, 0)  13.3 us
    ppermute x3, waiting for transfers between devices, from_behind(): return lax.ppermute(value, axis, pairs)  12.6 us
    ppermute x3, starting transfers between devices, from_behind(): return lax.ppermute(value, axis, pairs)  8.72 us
    psum x1, blocking collectives, local(): lists = lax.psum(mine, 'grp')  8.09 us
    pallas_call x1, Pallas kernels, local(): pl.pallas_call(pair_kernel, out_shape=fields, in_specs=[smem] * 2 + [vmem...  2.66 us
  transfers between devices with their start and end apart: 3, of which 2 were waited for; matrix products, arithmetic and copies ran while one was open for 0% of the time, Pallas kernels for 3%

profile of v6, /device:TPU:2, one launch (start us, length us, event | category | flops | bytes accessed | tf_op | source)
XLA Modules:
  0.0 64.7 jit_solution(982935344380601547)
XLA Ops:
  0.0 0.0 copy-start.8
  0.0 0.0 copy-start.7
  0.7 0.0 copy-done.8
  0.7 0.0 copy-done.7
  0.7 0.1 entry.1
  0.8 1.9 %collective-permute-start = (s32[4,1,128]{2,1,0:T(1,128)S(1)}, s32[4,1,128]{2,1,0:T(1,128)S(1)}, u32[]{:S(2)}, u32[]{:S(2)}) collective-permute-start(s32[4,1,128]{2,1,0:T(1,128)S(1)} %entry.1), channel_id=1, source_target_pairs={{0,4},{4,8},{8,12},{12,16},{16,20},{20,24},{24,28},{28,32},{32,36}... | collective-permute-start | bytes 6152 | tf_op jit(solution)/shard_map/ppermute | solution.py:65
  2.7 3.6 %collective-permute-start.1 = (f32[6,2,8,1024]{3,2,1,0:T(8,128)}, f32[6,2,8,1024]{3,2,1,0:T(8,128)S(1)}, u32[]{:S(2)}, u32[]{:S(2)}) collective-permute-start(f32[6,2,8,1024]{3,2,1,0:T(8,128)} %source.1), channel_id=1, source_target_pairs={{0,4},{4,8},{8,12},{12,16},{16,20},{20,24},{24,28},{28,32},{32,36}... | collective-permute-start | bytes 1179656 | tf_op jit(solution)/shard_map/ppermute | solution.py:65
  6.3 1.0 %stage.1.here = f32[6,2,8,1024]{3,2,1,0:T(8,128)S(1)} custom-call(f32[6,2,8,1024]{3,2,1,0:T(8,128)} %source.1), custom_call_target="tpu_custom_call" | custom-call | flops 10000000000 | bytes 1048576 | tf_op jit(solution)/shard_map/stage/pallas_call | solution.py:334
  7.3 8.0 %collective-permute-done = s32[4,1,128]{2,1,0:T(1,128)S(1)} collective-permute-done((s32[4,1,128]{2,1,0:T(1,128)S(1)}, s32[4,1,128]{2,1,0:T(1,128)S(1)}, u32[]{:S(2)}, u32[]{:S(2)}) %collective-permute-start) | collective-permute-done | bytes 2080 | tf_op jit(solution)/shard_map/ppermute | solution.py:65
  15.3 8.1 %psum.7.lists = s32[4,1,128]{2,1,0:T(1,128)S(1)} all-reduce(s32[4,1,128]{2,1,0:T(1,128)S(1)} %collective-permute-done), channel_id=1, replica_groups=mesh['orb'=128,'grp'=4] {'grp'}, use_global_device_ids=true, to_apply=%region_0.0 | all-reduce | flops 512 | bytes 4096 | tf_op jit(solution)/shard_map/psum | solution.py:331
  23.4 0.0 collective-permute-done.1.behind
  23.4 0.7 %pack.1 = f32[4,4,2,8,1024]{4,3,2,1,0:T(8,128)S(1)} custom-call(s32[4,1,128]{2,1,0:T(1,128)S(1)} %psum.7.lists, f32[6,2,8,1024]{3,2,1,0:T(8,128)S(1)} %collective-permute-done.1.behind, f32[6,2,8,1024]{3,2,1,0:T(8,128)S(1)} %stage.1.here), custom_call_target="tpu_custom_call" | custom-call | tf_op jit(solution)/shard_map/pack/pallas_call | solution.py:343
  24.2 0.0 copy-start
  24.2 0.0 copy-start.1
  24.2 0.0 copy-start.2
  24.2 0.0 copy-start.3
  24.2 0.0 copy-start.4
  24.2 0.0 copy-start.5
  24.2 0.0 copy-start.6
  24.3 14.4 %all_to_all.10.got = f32[4,4,2,8,1024]{4,3,2,1,0:T(8,128)S(1)} all-to-all(f32[4,4,2,8,1024]{4,3,2,1,0:T(8,128)S(1)} %pack.1), channel_id=1, replica_groups=mesh['orb'=128,'grp'=4] {'grp'}, dimensions={0} | all-to-all | bytes 2097152 | tf_op jit(solution)/shard_map/all_to_all | solution.py:351
  38.6 0.0 copy-done
  38.6 0.0 copy-done.1
  38.6 0.0 copy-done.2
  38.6 0.0 copy-done.3
  38.6 0.0 copy-done.4
  38.6 0.0 copy-done.5
  38.7 0.0 copy-done.6
  38.7 2.7 %pairs.1 = f32[4,4,2,8,1024]{4,3,2,1,0:T(8,128)S(1)} custom-call(s32[3,768]{1,0:T(4,128)S(1)} %copy-done.4, s32[4,1,128]{2,1,0:T(1,128)S(1)} %psum.7.lists, f32[4,4,2,8,1024]{4,3,2,1,0:T(8,128)S(1)} %all_to_all.10.got, bf16[64,96]{1,0:T(8,128)(2,1)S(1)} %copy-done.3, bf16[768,256]{1,0:T(8,128)(2,1)S(1)} %copy-done.1, bf16[768,256]{1,0:T(8,128)(2,1)S(1)} %copy-done, ...), custom_call_target="tpu_custom_call" | custom-call | tf_op jit(solution)/shard_map/pairs/pallas_call | solution.py:354
  41.3 13.3 %all_to_all.11.got = f32[4,4,2,8,1024]{4,3,2,1,0:T(8,128)S(1)} all-to-all(f32[4,4,2,8,1024]{4,3,2,1,0:T(8,128)S(1)} %pairs.1), channel_id=1, replica_groups=mesh['orb'=128,'grp'=4] {'grp'}, dimensions={0} | all-to-all | bytes 2097152 | tf_op jit(solution)/shard_map/all_to_all | solution.py:363
  54.7 0.8 %back_terms.1 = f32[6,2,8,1024]{3,2,1,0:T(8,128)S(1)} custom-call(s32[4,1,128]{2,1,0:T(1,128)S(1)} %psum.7.lists, f32[4,4,2,8,1024]{4,3,2,1,0:T(8,128)S(1)} %all_to_all.11.got), custom_call_target="tpu_custom_call" | custom-call | tf_op jit(solution)/shard_map/back_terms/pallas_call | solution.py:365
  55.4 3.2 %collective-permute-start.2 = (f32[6,2,8,1024]{3,2,1,0:T(8,128)S(1)}, f32[6,2,8,1024]{3,2,1,0:T(8,128)S(1)}, u32[]{:S(2)}, u32[]{:S(2)}) collective-permute-start(f32[6,2,8,1024]{3,2,1,0:T(8,128)S(1)} %back_terms.1), channel_id=1, source_target_pairs={{0,508},{4,0},{8,4},{12,8},{16,12},{20,16},{24,20},{28,24},{32,28}... | collective-permute-start | bytes 1179656 | tf_op jit(solution)/shard_map/ppermute | solution.py:65
  58.6 0.7 %here_terms.1 = f32[6,2,8,1024]{3,2,1,0:T(8,128)S(1)} custom-call(s32[4,1,128]{2,1,0:T(1,128)S(1)} %psum.7.lists, f32[4,4,2,8,1024]{4,3,2,1,0:T(8,128)S(1)} %all_to_all.11.got), custom_call_target="tpu_custom_call" | custom-call | tf_op jit(solution)/shard_map/here_terms/pallas_call | solution.py:374
  59.3 4.6 %collective-permute-done.2 = f32[6,2,8,1024]{3,2,1,0:T(8,128)S(1)} collective-permute-done((f32[6,2,8,1024]{3,2,1,0:T(8,128)S(1)}, f32[6,2,8,1024]{3,2,1,0:T(8,128)S(1)}, u32[]{:S(2)}, u32[]{:S(2)}) %collective-permute-start.2) | collective-permute-done | bytes 393248 | tf_op jit(solution)/shard_map/ppermute | solution.py:65
  63.9 0.8 %add.5 = f32[6,2,8,1024]{3,2,1,0:T(8,128)} add(f32[6,2,8,1024]{3,2,1,0:T(8,128)S(1)} %here_terms.1, f32[6,2,8,1024]{3,2,1,0:T(8,128)S(1)} %collective-permute-done.2) | non-fusion elementwise | flops 98304 | bytes 1179648 | tf_op jit(solution)/shard_map/add | solution.py:382
Async XLA Ops:
  0.0 0.7 %copy-start.8 = (s32[1,1,2]{2,1,0:T(1,128)S(1)}, s32[1,1,2]{2,1,0:T(1,128)}, u32[]{:S(2)}) copy-start(s32[1,1,2]{2,1,0:T(1,128)} %seconds.1) | copy-start | bytes 28
  0.0 0.7 %copy-start.7 = (s32[1,1,2]{2,1,0:T(1,128)S(1)}, s32[1,1,2]{2,1,0:T(1,128)}, u32[]{:S(2)}) copy-start(s32[1,1,2]{2,1,0:T(1,128)} %firsts.1) | copy-start | bytes 28
  0.8 14.6 %collective-permute-start = (s32[4,1,128]{2,1,0:T(1,128)S(1)}, s32[4,1,128]{2,1,0:T(1,128)S(1)}, u32[]{:S(2)}, u32[]{:S(2)}) collective-permute-start(s32[4,1,128]{2,1,0:T(1,128)S(1)} %entry.1), channel_id=1, source_target_pairs={{0,4},{4,8},{8,12},{12,16},{16,20},{20,24},{24,28},{28,32},{32,36}... | collective-permute-start | bytes 6152 | tf_op jit(solution)/shard_map/ppermute | solution.py:65
  2.7 20.7 %collective-permute-start.1 = (f32[6,2,8,1024]{3,2,1,0:T(8,128)}, f32[6,2,8,1024]{3,2,1,0:T(8,128)S(1)}, u32[]{:S(2)}, u32[]{:S(2)}) collective-permute-start(f32[6,2,8,1024]{3,2,1,0:T(8,128)} %source.1), channel_id=1, source_target_pairs={{0,4},{4,8},{8,12},{12,16},{16,20},{20,24},{24,28},{28,32},{32,36}... | collective-permute-start | bytes 1179656 | tf_op jit(solution)/shard_map/ppermute | solution.py:65
  24.2 14.5 %copy-start = (bf16[768,256]{1,0:T(8,128)(2,1)S(1)}, bf16[768,256]{1,0:T(8,128)(2,1)}, u32[]{:S(2)}) copy-start(bf16[768,256]{1,0:T(8,128)(2,1)} %constant.14.clone.back3) | copy-start | bytes 1179652
  24.2 14.4 %copy-start.1 = (bf16[768,256]{1,0:T(8,128)(2,1)S(1)}, bf16[768,256]{1,0:T(8,128)(2,1)}, u32[]{:S(2)}) copy-start(bf16[768,256]{1,0:T(8,128)(2,1)} %constant.13.clone.for3) | copy-start | bytes 1179652
  24.2 14.4 %copy-start.2 = (f32[256,128]{1,0:T(8,128)S(1)}, f32[256,128]{1,0:T(8,128)}, u32[]{:S(2)}) copy-start(f32[256,128]{1,0:T(8,128)} %constant.17.clone.green) | copy-start | bytes 393220
  24.2 14.4 %copy-start.3 = (bf16[64,96]{1,0:T(8,128)(2,1)S(1)}, bf16[64,96]{1,0:T(8,128)(2,1)}, u32[]{:S(2)}) copy-start(bf16[64,96]{1,0:T(8,128)(2,1)} %constant.12.clone.left3) | copy-start | bytes 36868
  24.2 14.4 %copy-start.4 = (s32[3,768]{1,0:T(4,128)S(1)}, s32[3,768]{1,0:T(4,128)}, u32[]{:S(2)}) copy-start(s32[3,768]{1,0:T(4,128)} %offsets.1) | copy-start | bytes 27652
  24.2 14.4 %copy-start.5 = (f32[8,128]{1,0:T(8,128)S(1)}, f32[8,128]{1,0:T(8,128)}, u32[]{:S(2)}) copy-start(f32[8,128]{1,0:T(8,128)} %constant.16.clone.twid_im) | copy-start | bytes 12292
  24.2 14.4 %copy-start.6 = (f32[8,128]{1,0:T(8,128)S(1)}, f32[8,128]{1,0:T(8,128)}, u32[]{:S(2)}) copy-start(f32[8,128]{1,0:T(8,128)} %constant.15.clone.twid_re) | copy-start | bytes 12292
  55.4 8.5 %collective-permute-start.2 = (f32[6,2,8,1024]{3,2,1,0:T(8,128)S(1)}, f32[6,2,8,1024]{3,2,1,0:T(8,128)S(1)}, u32[]{:S(2)}, u32[]{:S(2)}) collective-permute-start(f32[6,2,8,1024]{3,2,1,0:T(8,128)S(1)} %back_terms.1), channel_id=1, source_target_pairs={{0,508},{4,0},{8,4},{12,8},{16,12},{20,16},{24,20},{28,24},{32,28}... | collective-permute-start | bytes 1179656 | tf_op jit(solution)/shard_map/ppermute | solution.py:65

commit v7 on v6

--- a/solution.py
+++ b/solution.py
@@ -327,7 +327,6 @@
         name="entry",
     )(pair_first, pair_second, pair_count)
     mine = from_behind(mine, "orb", 1)
-    behind = from_behind(orbitals, "orb", 1)
     lists = lax.psum(mine, "grp")
     slots = 2 * PAIRS
     fields = jax.ShapeDtypeStruct((members, slots, 2, rows, CELLS), F32)
@@ -340,6 +339,7 @@
         cost_estimate=pl.CostEstimate(flops=10**10, bytes_accessed=1 << 20, transcendentals=0),
         name="stage",
     )(pltpu.with_memory_space_constraint(orbitals, pltpu.HBM))
+    behind = from_behind(here, "orb", 1)
     packed = pl.pallas_call(
         pack_kernel,
         out_shape=fields,

time: 65 us -> 69.6 us (1.071)
  waiting for transfers between devices: 12.6 us -> 17.1 us
  blocking collectives: 35.8 us -> 37.1 us
  starting transfers between devices: 8.72 us -> 7.55 us
    ppermute x3, waiting for transfers between devices: 12.6 us -> 17.1 us  [from_behind(): return lax.ppermute(value, axis, pairs)]
    all_to_all x1, blocking collectives: 14.4 us -> 15.7 us  [local(): got = lax.all_to_all(packed, 'grp', 0, 0)]
    ppermute x3, starting transfers between devices: 8.72 us -> 7.55 us  [from_behind(): return lax.ppermute(value, axis, pairs)]
  transfers between devices with their start and end apart: 3 -> 3, of which waited for: 2 -> 2; matrix products, arithmetic and copies ran while one was open for 0% -> 0% of each run, Pallas kernels for 3% -> 1%
where the time goes in v7:
time: 69.6 us; the launch traced here: 69.3 us
  blocking collectives  37.1 us (53%)
  waiting for transfers between devices  17.1 us (25%)
  starting transfers between devices  7.55 us (11%)
  Pallas kernels  5.92 us (9%)
  between operations  0.82 us (1%)
  other arithmetic  0.79 us (1%)
    ppermute x3, waiting for transfers between devices, from_behind(): return lax.ppermute(value, axis, pairs)  17.1 us
    all_to_all x1, blocking collectives, local(): got = lax.all_to_all(packed, 'grp', 0, 0)  15.7 us
    all_to_all x1, blocking collectives, local(): returned = lax.all_to_all(terms, 'grp', 0, 0)  13.3 us
    psum x1, blocking collectives, local(): lists = lax.psum(mine, 'grp')  8.1 us
    ppermute x3, starting transfers between devices, from_behind(): return lax.ppermute(value, axis, pairs)  7.55 us
    pallas_call x1, Pallas kernels, local(): pl.pallas_call(pair_kernel, out_shape=fields, in_specs=[smem] * 2 + [vmem...  2.67 us
  transfers between devices with their start and end apart: 3, of which 2 were waited for; matrix products, arithmetic and copies ran while one was open for 0% of the time, Pallas kernels for 1%

profile of v7, /device:TPU:2, one launch (start us, length us, event | category | flops | bytes accessed | tf_op | source)
XLA Modules:
  0.0 69.3 jit_solution(6589608333664064895)
XLA Ops:
  0.0 1.0 %stage.1.here = f32[6,2,8,1024]{3,2,1,0:T(8,128)S(1)} custom-call(f32[6,2,8,1024]{3,2,1,0:T(8,128)} %source.1), custom_call_target="tpu_custom_call" | custom-call | flops 10000000000 | bytes 1048576 | tf_op jit(solution)/shard_map/stage/pallas_call | solution.py:333
  1.0 0.0 copy-start.7
  1.0 0.0 copy-start.8
  1.0 2.0 %collective-permute-start.1 = (f32[6,2,8,1024]{3,2,1,0:T(8,128)S(1)}, f32[6,2,8,1024]{3,2,1,0:T(8,128)S(1)}, u32[]{:S(2)}, u32[]{:S(2)}) collective-permute-start(f32[6,2,8,1024]{3,2,1,0:T(8,128)S(1)} %stage.1.here), channel_id=1, source_target_pairs={{0,4},{4,8},{8,12},{12,16},{16,20},{20,24},{24,28},{28,32},{32,36}... | collective-permute-start | bytes 1179656 | tf_op jit(solution)/shard_map/ppermute | solution.py:65
  3.7 0.0 copy-done.7
  3.7 0.0 copy-done.8
  3.7 0.1 entry.1
  3.8 3.6 %collective-permute-start = (s32[4,1,128]{2,1,0:T(1,128)S(1)}, s32[4,1,128]{2,1,0:T(1,128)S(1)}, u32[]{:S(2)}, u32[]{:S(2)}) collective-permute-start(s32[4,1,128]{2,1,0:T(1,128)S(1)} %entry.1), channel_id=1, source_target_pairs={{0,4},{4,8},{8,12},{12,16},{16,20},{20,24},{24,28},{28,32},{32,36}... | collective-permute-start | bytes 6152 | tf_op jit(solution)/shard_map/ppermute | solution.py:65
  7.4 12.5 %collective-permute-done = s32[4,1,128]{2,1,0:T(1,128)S(1)} collective-permute-done((s32[4,1,128]{2,1,0:T(1,128)S(1)}, s32[4,1,128]{2,1,0:T(1,128)S(1)}, u32[]{:S(2)}, u32[]{:S(2)}) %collective-permute-start) | collective-permute-done | bytes 2080 | tf_op jit(solution)/shard_map/ppermute | solution.py:65
  19.9 8.1 %psum.7.lists = s32[4,1,128]{2,1,0:T(1,128)S(1)} all-reduce(s32[4,1,128]{2,1,0:T(1,128)S(1)} %collective-permute-done), channel_id=1, replica_groups=mesh['orb'=128,'grp'=4] {'grp'}, use_global_device_ids=true, to_apply=%region_0.0 | all-reduce | flops 512 | bytes 4096 | tf_op jit(solution)/shard_map/psum | solution.py:330
  28.0 0.0 collective-permute-done.1.behind
  28.0 0.7 %pack.1 = f32[4,4,2,8,1024]{4,3,2,1,0:T(8,128)S(1)} custom-call(s32[4,1,128]{2,1,0:T(1,128)S(1)} %psum.7.lists, f32[6,2,8,1024]{3,2,1,0:T(8,128)S(1)} %collective-permute-done.1.behind, f32[6,2,8,1024]{3,2,1,0:T(8,128)S(1)} %stage.1.here), custom_call_target="tpu_custom_call" | custom-call | tf_op jit(solution)/shard_map/pack/pallas_call | solution.py:343
  28.7 0.0 copy-start
  28.7 0.0 copy-start.1
  28.7 0.0 copy-start.2
  28.8 0.0 copy-start.3
  28.8 0.0 copy-start.4
  28.8 0.0 copy-start.5
  28.8 0.0 copy-start.6
  28.8 15.7 %all_to_all.10.got = f32[4,4,2,8,1024]{4,3,2,1,0:T(8,128)S(1)} all-to-all(f32[4,4,2,8,1024]{4,3,2,1,0:T(8,128)S(1)} %pack.1), channel_id=1, replica_groups=mesh['orb'=128,'grp'=4] {'grp'}, dimensions={0} | all-to-all | bytes 2097152 | tf_op jit(solution)/shard_map/all_to_all | solution.py:351
  44.5 0.0 copy-done
  44.5 0.0 copy-done.1
  44.5 0.0 copy-done.2
  44.5 0.0 copy-done.3
  44.5 0.0 copy-done.4
  44.5 0.0 copy-done.5
  44.5 0.0 copy-done.6
  44.5 2.7 %pairs.1 = f32[4,4,2,8,1024]{4,3,2,1,0:T(8,128)S(1)} custom-call(s32[3,768]{1,0:T(4,128)S(1)} %copy-done.4, s32[4,1,128]{2,1,0:T(1,128)S(1)} %psum.7.lists, f32[4,4,2,8,1024]{4,3,2,1,0:T(8,128)S(1)} %all_to_all.10.got, bf16[64,96]{1,0:T(8,128)(2,1)S(1)} %copy-done.3, bf16[768,256]{1,0:T(8,128)(2,1)S(1)} %copy-done.1, bf16[768,256]{1,0:T(8,128)(2,1)S(1)} %copy-done, ...), custom_call_target="tpu_custom_call" | custom-call | tf_op jit(solution)/shard_map/pairs/pallas_call | solution.py:354
  47.2 13.3 %all_to_all.11.got = f32[4,4,2,8,1024]{4,3,2,1,0:T(8,128)S(1)} all-to-all(f32[4,4,2,8,1024]{4,3,2,1,0:T(8,128)S(1)} %pairs.1), channel_id=1, replica_groups=mesh['orb'=128,'grp'=4] {'grp'}, dimensions={0} | all-to-all | bytes 2097152 | tf_op jit(solution)/shard_map/all_to_all | solution.py:363
  60.5 0.8 %back_terms.1 = f32[6,2,8,1024]{3,2,1,0:T(8,128)S(1)} custom-call(s32[4,1,128]{2,1,0:T(1,128)S(1)} %psum.7.lists, f32[4,4,2,8,1024]{4,3,2,1,0:T(8,128)S(1)} %all_to_all.11.got), custom_call_target="tpu_custom_call" | custom-call | tf_op jit(solution)/shard_map/back_terms/pallas_call | solution.py:365
  61.3 1.9 %collective-permute-start.2 = (f32[6,2,8,1024]{3,2,1,0:T(8,128)S(1)}, f32[6,2,8,1024]{3,2,1,0:T(8,128)S(1)}, u32[]{:S(2)}, u32[]{:S(2)}) collective-permute-start(f32[6,2,8,1024]{3,2,1,0:T(8,128)S(1)} %back_terms.1), channel_id=1, source_target_pairs={{0,508},{4,0},{8,4},{12,8},{16,12},{20,16},{24,20},{28,24},{32,28}... | collective-permute-start | bytes 1179656 | tf_op jit(solution)/shard_map/ppermute | solution.py:65
  63.2 0.7 %here_terms.1 = f32[6,2,8,1024]{3,2,1,0:T(8,128)S(1)} custom-call(s32[4,1,128]{2,1,0:T(1,128)S(1)} %psum.7.lists, f32[4,4,2,8,1024]{4,3,2,1,0:T(8,128)S(1)} %all_to_all.11.got), custom_call_target="tpu_custom_call" | custom-call | tf_op jit(solution)/shard_map/here_terms/pallas_call | solution.py:374
  63.9 4.6 %collective-permute-done.2 = f32[6,2,8,1024]{3,2,1,0:T(8,128)S(1)} collective-permute-done((f32[6,2,8,1024]{3,2,1,0:T(8,128)S(1)}, f32[6,2,8,1024]{3,2,1,0:T(8,128)S(1)}, u32[]{:S(2)}, u32[]{:S(2)}) %collective-permute-start.2) | collective-permute-done | bytes 393248 | tf_op jit(solution)/shard_map/ppermute | solution.py:65
  68.5 0.8 %add.5 = f32[6,2,8,1024]{3,2,1,0:T(8,128)} add(f32[6,2,8,1024]{3,2,1,0:T(8,128)S(1)} %here_terms.1, f32[6,2,8,1024]{3,2,1,0:T(8,128)S(1)} %collective-permute-done.2) | non-fusion elementwise | flops 98304 | bytes 1179648 | tf_op jit(solution)/shard_map/add | solution.py:382
Async XLA Ops:
  1.0 2.7 %copy-start.7 = (s32[1,1,2]{2,1,0:T(1,128)S(1)}, s32[1,1,2]{2,1,0:T(1,128)}, u32[]{:S(2)}) copy-start(s32[1,1,2]{2,1,0:T(1,128)} %firsts.1) | copy-start | bytes 28
  1.0 2.7 %copy-start.8 = (s32[1,1,2]{2,1,0:T(1,128)S(1)}, s32[1,1,2]{2,1,0:T(1,128)}, u32[]{:S(2)}) copy-start(s32[1,1,2]{2,1,0:T(1,128)} %seconds.1) | copy-start | bytes 28
  1.0 27.0 %collective-permute-start.1 = (f32[6,2,8,1024]{3,2,1,0:T(8,128)S(1)}, f32[6,2,8,1024]{3,2,1,0:T(8,128)S(1)}, u32[]{:S(2)}, u32[]{:S(2)}) collective-permute-start(f32[6,2,8,1024]{3,2,1,0:T(8,128)S(1)} %stage.1.here), channel_id=1, source_target_pairs={{0,4},{4,8},{8,12},{12,16},{16,20},{20,24},{24,28},{28,32},{32,36}... | collective-permute-start | bytes 1179656 | tf_op jit(solution)/shard_map/ppermute | solution.py:65
  3.8 16.1 %collective-permute-start = (s32[4,1,128]{2,1,0:T(1,128)S(1)}, s32[4,1,128]{2,1,0:T(1,128)S(1)}, u32[]{:S(2)}, u32[]{:S(2)}) collective-permute-start(s32[4,1,128]{2,1,0:T(1,128)S(1)} %entry.1), channel_id=1, source_target_pairs={{0,4},{4,8},{8,12},{12,16},{16,20},{20,24},{24,28},{28,32},{32,36}... | collective-permute-start | bytes 6152 | tf_op jit(solution)/shard_map/ppermute | solution.py:65
  28.7 15.8 %copy-start = (bf16[768,256]{1,0:T(8,128)(2,1)S(1)}, bf16[768,256]{1,0:T(8,128)(2,1)}, u32[]{:S(2)}) copy-start(bf16[768,256]{1,0:T(8,128)(2,1)} %constant.14.clone.back3) | copy-start | bytes 1179652
  28.7 15.7 %copy-start.1 = (bf16[768,256]{1,0:T(8,128)(2,1)S(1)}, bf16[768,256]{1,0:T(8,128)(2,1)}, u32[]{:S(2)}) copy-start(bf16[768,256]{1,0:T(8,128)(2,1)} %constant.13.clone.for3) | copy-start | bytes 1179652
  28.7 15.7 %copy-start.2 = (f32[256,128]{1,0:T(8,128)S(1)}, f32[256,128]{1,0:T(8,128)}, u32[]{:S(2)}) copy-start(f32[256,128]{1,0:T(8,128)} %constant.17.clone.green) | copy-start | bytes 393220
  28.8 15.7 %copy-start.3 = (bf16[64,96]{1,0:T(8,128)(2,1)S(1)}, bf16[64,96]{1,0:T(8,128)(2,1)}, u32[]{:S(2)}) copy-start(bf16[64,96]{1,0:T(8,128)(2,1)} %constant.12.clone.left3) | copy-start | bytes 36868
  28.8 15.7 %copy-start.4 = (s32[3,768]{1,0:T(4,128)S(1)}, s32[3,768]{1,0:T(4,128)}, u32[]{:S(2)}) copy-start(s32[3,768]{1,0:T(4,128)} %offsets.1) | copy-start | bytes 27652
  28.8 15.7 %copy-start.5 = (f32[8,128]{1,0:T(8,128)S(1)}, f32[8,128]{1,0:T(8,128)}, u32[]{:S(2)}) copy-start(f32[8,128]{1,0:T(8,128)} %constant.16.clone.twid_im) | copy-start | bytes 12292
  28.8 15.7 %copy-start.6 = (f32[8,128]{1,0:T(8,128)S(1)}, f32[8,128]{1,0:T(8,128)}, u32[]{:S(2)}) copy-start(f32[8,128]{1,0:T(8,128)} %constant.15.clone.twid_re) | copy-start | bytes 12292
  61.3 7.2 %collective-permute-start.2 = (f32[6,2,8,1024]{3,2,1,0:T(8,128)S(1)}, f32[6,2,8,1024]{3,2,1,0:T(8,128)S(1)}, u32[]{:S(2)}, u32[]{:S(2)}) collective-permute-start(f32[6,2,8,1024]{3,2,1,0:T(8,128)S(1)} %back_terms.1), channel_id=1, source_target_pairs={{0,508},{4,0},{8,4},{12,8},{16,12},{20,16},{24,20},{28,24},{32,28}... | collective-permute-start | bytes 1179656 | tf_op jit(solution)/shard_map/ppermute | solution.py:65
